TPU v7x, 512 devices: a whole 4x8x8 slice. The times are simulated.
512 devices in a mesh: row: 32 (over z, x), col: 16 (over y, core).
Axes of the slice: x: 4, y: 8, z: 8, core: 2. Of those that a mesh axis runs over, the one named last changes fastest.
Arguments:
- tiles: float32 [8192, 128, 128], P(('row', 'col')), may hold values from -1 to 1
- coords: int32 [8192, 2], P(('row', 'col')), may hold values from 0 to 4095, as said below
- counts: int32 [512], P(('row', 'col')), may hold values from 8 to 16
- probes: bfloat16 [64, 16, 32768], P(None, 'col', 'row'), may hold values from -6 to 6
Outputs:
- q_basis: float32 [64, 131072], P(None, ('row', 'col'))
- w_basis: bfloat16 [64, 16, 32768], P(None, 'col', 'row')
- r_factor: float32 [64, 64], replicated
Inputs may be any that keep to these rules, and one draw needn't show every extreme that they name: `coords`: slots are ordered by device, row index first, 16 slots a device. The slots of device (r, c) name block rows r * 32 to (r + 1) * 32 - 1 and block columns c * 256 to (c + 1) * 256 - 1. Shares are the aligned runs of 8 block columns. Among the live slots of one device at most 1 name block columns of one share. Pairs may repeat; their tiles then add.
All inputs are finite; a program needn't handle non-finite values.
Results may differ from a plain program's by a relative error of at most 0.0012.
Values may be sent and summed in bfloat16 or wider, within the bound.
A program may use at most 64 MiB of HBM per device.

v0:
```python
import jax
import jax.numpy as jnp
from jax import lax
from jax.sharding import PartitionSpec as P

RB_DEV = 32


highest = lax.Precision.HIGHEST


def lower_inverse(lower):
    size = lower.shape[0]
    ident = jnp.eye(size, dtype=jnp.float32)
    return jax.scipy.linalg.solve_triangular(lower, ident, lower=True)


def product(left, right):
    return jnp.dot(left, right, preferred_element_type=jnp.float32, precision=highest)


def shards(tiles, coords, counts, probes):
    n_row = lax.axis_size("row")
    n_col = lax.axis_size("col")
    capacity = tiles.shape[0]
    block = tiles.shape[1]
    probe_count = probes.shape[0]
    share = probes.shape[2]
    per_owner = share // block
    per_group = per_owner * n_row
    slots = (3 * capacity + 2 * n_row - 1) // (2 * n_row)
    group_rows = RB_DEV * block
    total_rows = group_rows * n_row
    total_cols = share * n_row * n_col
    order = jnp.arange(capacity, dtype=jnp.int32)
    live = order < counts[0]
    weight = live.astype(jnp.float32)
    row_local = coords[:, 0] % RB_DEV
    col_local = coords[:, 1] % per_group
    owner = col_local // per_owner
    within = col_local % per_owner
    earlier = (owner[:, None] == owner[None, :]) & live[None, :] & (order[None, :] < order[:, None])
    rank = jnp.sum(earlier.astype(jnp.int32), axis=1)
    position = jnp.where(live, owner * slots + rank, n_row * slots)
    chosen = (position[:, None] == jnp.arange(n_row * slots, dtype=jnp.int32)[None, :]) & live[
        :, None
    ]
    filled = jnp.any(chosen, axis=0)
    source = jnp.sum(jnp.where(chosen, order[:, None], 0), axis=0)
    slot_ids = jnp.where(filled, within[source], per_owner)
    row_pick = (
        (row_local[:, None] == jnp.arange(RB_DEV, dtype=jnp.int32)[None, :]) & live[:, None]
    ).astype(jnp.float32)

    def fetch(own):
        strip = lax.all_gather(own, "row", axis=1, tiled=True).reshape(
            probe_count, per_group, block
        )
        return jnp.take(strip, col_local, axis=1)

    def sketch(blocks):
        contrib = jnp.einsum("ptk,tik->pti", blocks.astype(jnp.float32), tiles, precision=highest)
        summed = jnp.einsum("tr,pti->pri", row_pick, contrib, precision=highest)
        return summed.reshape(probe_count, group_rows)

    def reduce_rows(partial_rows):
        held = lax.psum_scatter(partial_rows, "col", scatter_dimension=1, tiled=True)
        gram = lax.psum(product(held, held.T), ("row", "col"))
        lower = jnp.linalg.cholesky(gram / total_rows)
        return (held, lower, lower_inverse(lower))

    first, lower_one, inverse_one = reduce_rows(sketch(fetch(probes.reshape(probe_count, share))))
    first = product(inverse_one, first)
    group = lax.all_gather(first, "col", axis=1, tiled=True)
    picked = jnp.take(group.reshape(probe_count, RB_DEV, block), row_local, axis=1)
    terms = jnp.einsum("pti,tik->tpk", picked, tiles, precision=highest) * weight[:, None, None]
    outgoing = jnp.take(terms, source, axis=0) * filled.astype(jnp.float32)[:, None, None]
    incoming, incoming_ids = (
        lax.all_to_all(outgoing, "row", split_axis=0, concat_axis=0, tiled=True),
        lax.all_to_all(slot_ids, "row", split_axis=0, concat_axis=0, tiled=True),
    )
    placed = (incoming_ids[:, None] == jnp.arange(per_owner, dtype=jnp.int32)[None, :]).astype(
        jnp.float32
    )
    column_part = jnp.einsum("sb,spk->pbk", placed, incoming, precision=highest).reshape(
        probe_count, share
    )
    gram_cols = lax.psum(product(column_part, column_part.T), ("row", "col"))
    lower_cols = jnp.linalg.cholesky(gram_cols / total_cols)
    basis = product(lower_inverse(lower_cols), column_part).astype(jnp.bfloat16)
    second, lower_two, inverse_two = reduce_rows(sketch(fetch(basis)))
    q_basis = product(inverse_two, second)
    return (q_basis, basis.reshape(probe_count, 1, share), lower_two.T)


def solution(mesh):
    in_specs = (
        P(("row", "col"), None, None),
        P(("row", "col"), None),
        P(("row", "col")),
        P(None, "col", "row"),
    )
    out_specs = (P(None, ("row", "col")), P(None, "col", "row"), P())
    return jax.shard_map(shards, mesh=mesh, in_specs=in_specs, out_specs=out_specs, check_vma=False)
```

profile of v0, /device:TPU:1, one launch (start us, length us, event | category | flops | bytes accessed | tf_op | source)
XLA Modules:
  0.0 751.5 jit_solution(11568969367112235923)
XLA Ops:
  10.1 91.7 %all-gather.9.cloned.1.call-done = bf16[64,1,32768]{2,0,1:T(8,128)(2,1)} async-done(((bf16[64,1,1024]{2,0,1:T(8,128)(2,1)}), bf16[64,1,32768]{2,0,1:T(8,128)(2,1)}) %all-gather.9.cloned.1.call-update) | async-done | bytes 4194320 | tf_op jit(solution)/shard_map/all_gather | solution.py:56
  101.7 3.3 copy.97
  105.1 4.6 copy.75
  109.7 2.8 gather_fusion.3
  112.5 1.2 convolution_bitcast_fusion.1
  114.6 1.6 copy.118
  116.3 57.6 %reduce-scatter.3.cloned.1.call-done = f32[64,256]{1,0:T(8,128)} async-done(((f32[64,4096]{1,0:T(8,128)}), f32[64,256]{1,0:T(8,128)}) %reduce-scatter.3.cloned.1.call-update) | async-done | bytes 65552 | tf_op jit(solution)/shard_map/reduce_scatter | solution.py:67
  173.9 1.1 fusion.65
  175.0 100.2 %psum.21 = f32[64,64]{0,1:T(8,128)S(1)} all-reduce(f32[64,64]{0,1:T(8,128)S(1)} %fusion.65), channel_id=1, replica_groups=mesh['row'=32,'col'=16] {'row','col'}, use_global_device_ids=true, to_apply=%region_3.5 | all-reduce | flops 4096 | bytes 32768 | tf_op jit(solution)/shard_map/psum | solution.py:68
  275.3 5.8 cholesky.59
  282.5 4.9 custom-call.7
  287.7 1.7 fusion.66
  291.2 4.7 all-to-all-start.1
  296.0 30.1 %all-gather.5.cloned.1.call-done = f32[64,4096]{1,0:T(8,128)} async-done(((f32[64,256]{1,0:T(8,128)}), f32[64,4096]{1,0:T(8,128)}) %all-gather.5.cloned.1.call-update) | async-done | bytes 1048592 | tf_op jit(solution)/shard_map/all_gather | solution.py:74
  326.1 1.3 copy_bitcast_fusion.3
  329.8 1.2 select_multiply_fusion
  331.0 9.9 %all-to-all-start = ((f32[32,64,128]{2,1,0:T(8,128)}), f32[32,64,128]{2,1,0:T(8,128)S(1)}, u32[]{:S(2)}, u32[]{:S(2)}) async-start(f32[32,64,128]{2,1,0:T(8,128)} %select_multiply_fusion), calls=%async_computation.1 | async-start | bytes 2097152 | tf_op jit(solution)/shard_map/all_to_all | solution.py:79
  341.6 26.2 %all-to-all-done = f32[32,64,128]{2,1,0:T(8,128)S(1)} async-done(((f32[32,64,128]{2,1,0:T(8,128)}), f32[32,64,128]{2,1,0:T(8,128)S(1)}, u32[]{:S(2)}, u32[]{:S(2)}) %all-to-all-start) | async-done | bytes 1048608 | tf_op jit(solution)/shard_map/all_to_all | solution.py:79
  369.2 96.7 %psum.22 = f32[64,64]{0,1:T(8,128)S(1)} all-reduce(f32[64,64]{0,1:T(8,128)S(1)} %convolution_bitcast_fusion.2), channel_id=1, replica_groups=mesh['row'=32,'col'=16] {'row','col'}, use_global_device_ids=true, to_apply=%region_7.11 | all-reduce | flops 4096 | bytes 32768 | tf_op jit(solution)/shard_map/psum | solution.py:88
  466.0 5.8 cholesky.70
  473.1 4.9 custom-call.8
  479.4 80.1 %all-gather.7.cloned.1.call-done = bf16[64,32768]{1,0:T(8,128)(2,1)} async-done(((bf16[64,1024]{1,0:T(8,128)(2,1)}), bf16[64,32768]{1,0:T(8,128)(2,1)}) %all-gather.7.cloned.1.call-update) | async-done | bytes 4194320 | tf_op jit(solution)/shard_map/all_gather | solution.py:56
  559.5 5.4 copy_bitcast_fusion
  564.9 2.8 gather_fusion.4
  567.6 1.2 convolution_bitcast_fusion
  569.7 1.6 copy.117
  571.3 57.7 %reduce-scatter.5.cloned.1.call-done = f32[64,256]{1,0:T(8,128)} async-done(((f32[64,4096]{1,0:T(8,128)}), f32[64,256]{1,0:T(8,128)}) %reduce-scatter.5.cloned.1.call-update) | async-done | bytes 65552 | tf_op jit(solution)/shard_map/reduce_scatter | solution.py:67
  629.0 1.1 fusion.67
  630.1 100.0 %psum.23 = f32[64,64]{0,1:T(8,128)S(1)} all-reduce(f32[64,64]{0,1:T(8,128)S(1)} %fusion.67), channel_id=1, replica_groups=mesh['row'=32,'col'=16] {'row','col'}, use_global_device_ids=true, to_apply=%region_9.13 | all-reduce | flops 4096 | bytes 32768 | tf_op jit(solution)/shard_map/psum | solution.py:68
  730.3 5.8 cholesky.81
  738.2 4.9 custom-call.9
  743.3 1.7 fusion.68
  (66 shorter events, 17.1 us)
Async XLA Ops:
  7.2 105.3 %copy-start = (f32[16,128,128]{2,1,0:T(8,128)S(1)}, f32[16,128,128]{2,1,0:T(8,128)}, u32[]{:S(2)}) copy-start(f32[16,128,128]{2,1,0:T(8,128)} %param.9) | copy-start | bytes 3145732
  7.2 94.5 %all-gather.9.cloned.1.call-start = ((), (), s32[]{:S(2)}) async-start(), calls=%async_computation.8 | async-start | bytes 4325376 | tf_op jit(solution)/shard_map/all_gather | solution.py:56
  7.9 166.0 %reduce-scatter.3.cloned.1.call-start = ((), (), s32[]{:S(2)}) async-start(), calls=%async_computation.4 | async-start | bytes 1114112 | tf_op jit(solution)/shard_map/reduce_scatter | solution.py:67
  109.7 179.7 %copy-start.1 = (s32[16,2]{0,1:T(2,128)S(1)}, s32[16,2]{0,1:T(2,128)}, u32[]{:S(2)}) copy-start(s32[16,2]{0,1:T(2,128)} %param.10) | copy-start | bytes 388
  116.2 209.9 %all-gather.5.cloned.1.call-start = ((), (), s32[]{:S(2)}) async-start(), calls=%async_computation.5 | async-start | bytes 1114112 | tf_op jit(solution)/shard_map/all_gather | solution.py:74
  291.2 39.8 %all-to-all-start.1 = ((s32[32,1,1]{2,1,0:T(1,128)}), s32[32,1,1]{2,1,0:T(1,128)S(1)}, u32[]{:S(2)}, u32[]{:S(2)}) async-start(s32[32,1,1]{2,1,0:T(1,128)} %copy.80), calls=%async_computation.2 | async-start | bytes 32768 | tf_op jit(solution)/shard_map/all_to_all | solution.py:80
  331.0 36.8 %all-to-all-start = ((f32[32,64,128]{2,1,0:T(8,128)}), f32[32,64,128]{2,1,0:T(8,128)S(1)}, u32[]{:S(2)}, u32[]{:S(2)}) async-start(f32[32,64,128]{2,1,0:T(8,128)} %select_multiply_fusion), calls=%async_computation.1 | async-start | bytes 2097152 | tf_op jit(solution)/shard_map/all_to_all | solution.py:79
  340.9 218.6 %all-gather.7.cloned.1.call-start = ((), (), s32[]{:S(2)}) async-start(), calls=%async_computation.6 | async-start | bytes 4325376 | tf_op jit(solution)/shard_map/all_gather | solution.py:56
  479.4 149.6 %reduce-scatter.5.cloned.1.call-start = ((), (), s32[]{:S(2)}) async-start(), calls=%async_computation.7 | async-start | bytes 1114112 | tf_op jit(solution)/shard_map/reduce_scatter | solution.py:67
Sparse Core Ops, SparseCore 0:
  11.2 90.4 all-gather.8
  116.3 57.5 reduce-scatter.2
  289.5 36.5 all-gather.4
  479.5 79.9 all-gather.6
  571.5 57.5 reduce-scatter.4
where the time goes:
time: 752 us
  waiting for transfers between devices  344 us (46%)
  blocking collectives  297 us (39%)
  other arithmetic  39.9 us (5%)
  local copies, waits for them, and re-layouts  27 us (4%)
  starting transfers between devices  14.8 us (2%)
  between operations  14.7 us (2%)
  matrix products  14 us (2%)
    psum x2, blocking collectives, reduce_rows(): gram = lax.psum(product(held, held.T), ('row', 'col'))  200 us
    all_gather x2, waiting for transfers between devices, fetch(): lax.all_gather(own, 'row', axis=1, tiled=True)  172 us
    reduce_scatter x2, waiting for transfers between devices, reduce_rows(): lax.psum_scatter(partial_rows, 'col', scatter_dimension=1, tiled=True)  115 us
    psum x1, blocking collectives, shards(): gram_cols = lax.psum(product(column_part, column_part.T), ('row', 'col'))  96.7 us
    all_gather x1, waiting for transfers between devices, shards(): group = lax.all_gather(first, 'col', axis=1, tiled=True)  30.1 us
    all_to_all x1, waiting for transfers between devices, shards(): lax.all_to_all(outgoing, 'row', split_axis=0, concat_axis=0, tiled=True)  26.2 us
    another operation x5, other arithmetic, lower_inverse(): return jax.scipy.linalg.solve_triangular(lower, ident, lower=True)  16 us
  transfers between devices with their start and end apart: 7, of which 6 were waited for; matrix products, arithmetic and copies ran while one was open for 1% of the time, Pallas kernels for 0%

commit v1 on v0

v1 whole, which is shorter than its diff:
```python
import functools

import jax
import jax.numpy as jnp
from jax import lax
from jax.experimental import pallas as pl
from jax.experimental.pallas import tpu as pltpu
from jax.sharding import PartitionSpec as P

MESH = pl.DeviceIdType.MESH
highest = lax.Precision.HIGHEST
f32 = jnp.float32
bf16 = jnp.bfloat16
LANE = 128
CORES = 2
CHUNKS = 2


def nn(left, right):
    return lax.dot_general(
        left, right, (((1,), (0,)), ((), ())), precision=highest, preferred_element_type=f32
    )


def nt(left, right):
    return lax.dot_general(
        left, right, (((1,), (1,)), ((), ())), precision=highest, preferred_element_type=f32
    )


def remote(src, dst, send, recv, device):
    return pltpu.make_async_remote_copy(
        src_ref=src,
        dst_ref=dst,
        send_sem=send,
        recv_sem=recv,
        device_id=device,
        device_id_type=MESH,
    )


def loop(lower, upper, body):
    def step(i, carry):
        body(i)
        return carry

    lax.fori_loop(lower, upper, step, 0)


def offset(k, n):
    step = (k + 1) // 2
    return n // 2 + step * (2 * lax.rem(k, 2) - 1)


def greet(n_row, n_col, row, col, with_row, with_col):
    barrier = pltpu.get_barrier_semaphore()
    count = 0
    if with_row:
        loop(
            1,
            n_row,
            lambda d: pl.semaphore_signal(
                barrier, inc=1, device_id=(lax.rem(row + d, n_row), col), device_id_type=MESH
            ),
        )
        count += n_row - 1
    if with_col:
        loop(
            1,
            n_col,
            lambda d: pl.semaphore_signal(
                barrier, inc=1, device_id=(row, lax.rem(col + d, n_col)), device_id_type=MESH
            ),
        )
        count += n_col - 1
    pl.semaphore_wait(barrier, count)


class Exchange:
    def __init__(self, n, me, source, dst, send, recv, device):
        self.n, self.me, self.source, self.dst = n, me, source, dst
        self.send, self.recv, self.device = send, recv, device

    def copy_to(self, peer):
        return remote(
            self.source(peer),
            self.dst.at[self.me],
            self.send.at[peer],
            self.recv.at[self.me],
            self.device(peer),
        )

    def copy_from(self, peer):
        return remote(
            self.source(peer),
            self.dst.at[peer],
            self.send.at[peer],
            self.recv.at[peer],
            self.device(peer),
        )

    def start(self):
        loop(
            0, self.n - 1, lambda k: self.copy_to(lax.rem(self.me + offset(k, self.n), self.n)).start()
        )

    def wait(self):
        loop(
            0,
            self.n - 1,
            lambda k: self.copy_from(lax.rem(self.me - offset(k, self.n) + self.n, self.n)).wait(),
        )


def sum_slots(ref, n):
    total = ref[0]
    for s in range(1, n):
        total = total + ref[s]
    return total


def pack_gram(block):
    size = block.shape[0]
    half = size // 2
    zero = jnp.zeros_like(block)
    return nt(block[:half], jnp.concatenate([block, zero], axis=0)) + nt(
        block[half:], jnp.concatenate([zero, block], axis=0)
    )


class GramSum:
    def __init__(self, sizes, row, col, r, tag):
        n_row, n_col, nx = sizes
        nz = n_row // nx
        z, x = row // nx, lax.rem(row, nx)
        self.nx, self.nz, self.nc, self.x, self.z, self.col = nx, nz, n_col, x, z, col
        get = lambda name: r[tag + name]
        self.part, self.gx, self.s1, self.gz = get("part"), get("gx"), get("s1"), get("gz")
        self.s2, self.gc, self.out = get("s2"), get("gc"), get("out")
        along_x = lambda p: (z * nx + p, col)
        along_z = lambda p: (p * nx + x, col)
        along_c = lambda p: (row, p)
        part, s1, s2, out = self.part, self.s1, self.s2, self.out
        self.first = Exchange(
            nx, x, lambda p: part.at[p], self.gx, get("x_send"), get("x_recv"), along_x
        )
        self.second = Exchange(nz, z, lambda p: s1, self.gz, get("z_send"), get("z_recv"), along_z)
        self.third = Exchange(
            n_col, col, lambda p: s2, self.gc, get("c_send"), get("c_recv"), along_c
        )
        self.last = Exchange(
            nx, x, lambda p: out.at[x], out, get("o_send"), get("o_recv"), along_x
        )

    def scatter_x(self, packed):
        depth = packed.shape[0] // self.nx
        for j in range(self.nx):
            self.part[j] = packed[j * depth : (j + 1) * depth]
        self.first.start()
        self.gx[self.x] = self.part[self.x]

    def sum_z(self):
        self.first.wait()
        self.s1[...] = sum_slots(self.gx, self.nx)
        self.second.start()
        self.gz[self.z] = self.s1[...]

    def sum_columns(self):
        self.second.wait()
        self.s2[...] = sum_slots(self.gz, self.nz)
        self.third.start()
        self.gc[self.col] = self.s2[...]

    def gather_x(self):
        self.third.wait()
        self.out[self.x] = sum_slots(self.gc, self.nc)
        self.last.start()

    def result(self):
        self.last.wait()
        return self.out[...].reshape(32, LANE)


def gram_scratch(sizes, tag):
    n_row, n_col, nx = sizes
    depth = 32 // nx
    nz = n_row // nx
    dma = pltpu.SemaphoreType.DMA
    named = {
        "part": pltpu.VMEM((nx, depth, LANE), f32),
        "gx": pltpu.VMEM((nx, depth, LANE), f32),
        "s1": pltpu.VMEM((depth, LANE), f32),
        "gz": pltpu.VMEM((nz, depth, LANE), f32),
        "s2": pltpu.VMEM((depth, LANE), f32),
        "gc": pltpu.VMEM((n_col, depth, LANE), f32),
        "out": pltpu.VMEM((nx, depth, LANE), f32),
        "x_send": dma((nx,)),
        "x_recv": dma((nx,)),
        "z_send": dma((nz,)),
        "z_recv": dma((nz,)),
        "c_send": dma((n_col,)),
        "c_recv": dma((n_col,)),
        "o_send": dma((nx,)),
        "o_recv": dma((nx,)),
    }
    return {tag + name: shape for name, shape in named.items()}


def pick(own, wanted):
    wanted = jnp.broadcast_to(wanted, (own.shape[0], LANE))
    total = jnp.zeros((own.shape[0], LANE), f32)
    for b in range(own.shape[1] // LANE):
        total = jnp.where(wanted == b + 1, own[:, b * LANE : (b + 1) * LANE].astype(f32), total)
    return total.astype(bf16)


class Spread:
    def __init__(self, n_row, row, col, chunks, r, tag):
        self.n_row, self.row, self.chunks = n_row, row, chunks
        self.wanted = r["wanted"]
        self.outgoing = [r[tag + "outgoing%d" % c] for c in range(chunks)]
        self.got = [r[tag + "got%d" % c] for c in range(chunks)]
        self.moves = [
            Exchange(
                n_row,
                row,
                functools.partial(lambda ref, p: ref.at[p], self.outgoing[c]),
                self.got[c],
                r[tag + "send%d" % c],
                r[tag + "recv%d" % c],
                lambda p: (p, col),
            )
            for c in range(chunks)
        ]

    def store(self, refs, place, block):
        rows = block.shape[0] // self.chunks
        for c in range(self.chunks):
            refs[c][place] = block[c * rows : (c + 1) * rows]

    def start(self, own_ref, ready=None):
        def serve(k):
            peer = lax.rem(self.row - offset(k, self.n_row) + self.n_row, self.n_row)
            if ready is not None:
                ready(peer)
            self.store(self.outgoing, peer, pick(own_ref[...], self.wanted[peer]))
            self.moves[0].copy_to(peer).start()

        loop(0, self.n_row - 1, serve)
        self.store(self.got, self.row, pick(own_ref[...], self.wanted[self.row]))

    def finish(self, c):
        def step(k):
            peer = lax.rem(self.row - offset(k, self.n_row) + self.n_row, self.n_row)
            self.moves[c].copy_from(peer).wait()
            if c + 1 < self.chunks:
                self.moves[c + 1].copy_to(peer).start()

        loop(0, self.n_row - 1, step)


def spread_scratch(n_row, chunks, width, tag):
    rows = width // chunks
    named = {}
    for c in range(chunks):
        named[tag + "outgoing%d" % c] = pltpu.VMEM((n_row, rows, LANE), bf16)
        named[tag + "got%d" % c] = pltpu.VMEM((n_row, rows, LANE), bf16)
        named[tag + "send%d" % c] = pltpu.SemaphoreType.DMA((n_row,))
        named[tag + "recv%d" % c] = pltpu.SemaphoreType.DMA((n_row,))
    return named


class RowSums:
    def __init__(self, n_col, row, col, c, r, tag):
        self.ny = ny = n_col // CORES
        self.n_col = n_col
        self.y, self.core = col // CORES, lax.rem(col, CORES)
        self.row, self.col = row, col
        self.other = col + 1 - 2 * self.core
        get = lambda name: r[tag + name + "%d" % c]
        self.terms, self.part, self.near = get("contrib"), get("rows"), get("near")
        self.near_send, self.near_recv = get("near_send"), get("near_recv")
        self.summed, self.far = get("summed"), get("far")
        self.shares = Exchange(
            ny,
            self.y,
            lambda p: self.summed.at[p],
            self.far,
            get("far_send"),
            get("far_recv"),
            self.same_core,
        )
        if tag + "group%d" % c in r:
            self.group = get("group")
            self.all_send, self.all_recv = get("all_send"), get("all_recv")
            self.pass_send, self.pass_recv = get("pass_send"), get("pass_recv")

    def same_core(self, p):
        return (self.row, p * CORES + self.core)

    def near_copy(self, t):
        return remote(
            self.part.at[t * CORES + (1 - self.core)],
            self.near.at[t],
            self.near_send.at[t],
            self.near_recv.at[t],
            (self.row, self.other),
        )

    def peer(self, k):
        return lax.rem(self.y + offset(k, self.ny), self.ny)

    def sketch(self, got, splits, info):
        capacity = splits[0].shape[0]
        dims = (((1,), (1,)), ((), ()))
        for t in range(capacity):
            block = got[info["owner"](t)]
            total = lax.dot_general(block, splits[2][t], dims, preferred_element_type=f32)
            total += lax.dot_general(block, splits[1][t], dims, preferred_element_type=f32)
            total += lax.dot_general(block, splits[0][t], dims, preferred_element_type=f32)
            self.terms[t] = total
        self.terms[capacity] = jnp.zeros(self.terms.shape[1:], f32)

        def chain(t):
            self.terms[t] = self.terms[t] + self.terms[info["before"](t)]

        loop(0, capacity, chain)

        def place(p):
            for j in range(2):
                self.part[p, j] = self.terms[info["last"](2 * p + j)]

        loop(0, self.n_col, place)

    def start(self):
        loop(0, self.ny - 1, lambda k: self.near_copy(self.peer(k)).start())
        self.near_copy(self.y).start()

    def pair_up(self):
        def step(k):
            peer = self.peer(k)
            self.near_copy(peer).wait()
            self.summed[peer] = self.part[peer * CORES + self.core] + self.near[peer]
            self.shares.copy_to(peer).start()

        loop(0, self.ny - 1, step)
        self.near_copy(self.y).wait()
        self.far[self.y] = self.part[self.y * CORES + self.core] + self.near[self.y]

    def total(self):
        self.shares.wait()
        return sum_slots(self.far, self.ny)

    def pass_copy(self, slot, peer):
        return remote(
            self.group.at[slot],
            self.group.at[slot],
            self.pass_send.at[peer],
            self.pass_recv.at[peer],
            (self.row, self.other),
        )

    def gather(self, total):
        self.group[self.col] = total
        mine = self.group.at[self.col]

        def send(k):
            peer = self.peer(k)
            remote(
                mine, mine, self.all_send.at[peer], self.all_recv.at[self.y], self.same_core(peer)
            ).start()

        loop(0, self.ny - 1, send)
        self.pass_copy(self.col, self.y).start()

    def gathered(self):
        def relay(k):
            peer = lax.rem(self.y - offset(k, self.ny) + self.ny, self.ny)
            slot = peer * CORES + self.core
            remote(
                self.group.at[self.col],
                self.group.at[slot],
                self.all_send.at[peer],
                self.all_recv.at[peer],
                self.same_core(peer),
            ).wait()
            self.pass_copy(slot, peer).start()

        loop(0, self.ny - 1, relay)
        loop(0, self.ny, lambda p: self.pass_copy(p * CORES + (1 - self.core), p).wait())


def row_scratch(n_col, capacity, chunks, width, tag, gather):
    ny = n_col // CORES
    rows = width // chunks
    dma = pltpu.SemaphoreType.DMA
    named = {}
    for c in range(chunks):
        some = {
            "contrib": pltpu.VMEM((capacity + 1, rows, LANE), f32),
            "rows": pltpu.VMEM((n_col, 2, rows, LANE), f32),
            "near": pltpu.VMEM((ny, 2, rows, LANE), f32),
            "summed": pltpu.VMEM((ny, 2, rows, LANE), f32),
            "far": pltpu.VMEM((ny, 2, rows, LANE), f32),
        }
        sems = ["near_send", "near_recv", "far_send", "far_recv"]
        if gather:
            some["group"] = pltpu.VMEM((n_col, 2, rows, LANE), f32)
            sems += ["all_send", "all_recv", "pass_send", "pass_recv"]
        for name in sems:
            some[name] = dma((ny,))
        for name, shape in some.items():
            named[tag + name + "%d" % c] = shape
    return named


def three(value):
    high = value.astype(bf16)
    rest = value - high.astype(f32)
    middle = rest.astype(bf16)
    return high, middle, (rest - middle.astype(f32)).astype(bf16)


class ColumnSums:
    def __init__(self, n_row, row, col, c, r):
        self.n_row, self.row = n_row, row
        self.terms, self.outgoing, self.arrived = (
            r["terms%d" % c],
            r["leaving%d" % c],
            r["arrived%d" % c],
        )
        self.wanted = r["wanted"]
        self.moved = Exchange(
            n_row,
            row,
            lambda p: self.outgoing.at[p],
            self.arrived,
            r["leaving_send%d" % c],
            r["leaving_recv%d" % c],
            lambda p: (p, col),
        )

    def start(self, group, splits, info):
        capacity = splits[0].shape[0]
        rows = self.terms.shape[1]

        def dot(left, right):
            return lax.dot_general(
                left, right, (((1,), (0,)), ((), ())), preferred_element_type=f32
            )

        for t in range(capacity):
            place = info["place"](t)
            source = group[place // 2, lax.rem(place, 2)]
            high, middle, low = three(source)
            by_high = dot(jnp.concatenate([high, middle, low], axis=0), splits[0][t])
            by_middle = dot(jnp.concatenate([high, middle], axis=0), splits[1][t])
            by_low = dot(high, splits[2][t])
            small = by_high[2 * rows :] + by_middle[rows:] + by_low
            self.terms[t] = by_high[:rows] + (by_high[rows : 2 * rows] + by_middle[:rows] + small)
        self.terms[capacity] = jnp.zeros(self.terms.shape[1:], f32)

        def serve(k):
            peer = lax.rem(self.row + offset(k, self.n_row), self.n_row)
            self.outgoing[peer] = self.terms[info["slot"](peer)]
            self.moved.copy_to(peer).start()

        loop(0, self.n_row - 1, serve)
        self.arrived[self.row] = self.terms[info["slot"](self.row)]

    def finish(self, columns_ref, first):
        self.moved.wait()
        rows = self.arrived.shape[1]

        def column(b):
            def add(s, total):
                hit = jnp.broadcast_to(self.wanted[s], (rows, LANE)) == b + 1
                return total + jnp.where(hit, self.arrived[s], 0.0)

            columns_ref[b, first : first + rows] = lax.fori_loop(
                0, self.n_row, add, jnp.zeros((rows, LANE), f32)
            )

        loop(0, columns_ref.shape[0], column)


def column_scratch(n_row, capacity, chunks, width):
    rows = width // chunks
    named = {}
    for c in range(chunks):
        named["terms%d" % c] = pltpu.VMEM((capacity + 1, rows, LANE), f32)
        named["leaving%d" % c] = pltpu.VMEM((n_row, rows, LANE), f32)
        named["arrived%d" % c] = pltpu.VMEM((n_row, rows, LANE), f32)
        named["leaving_send%d" % c] = pltpu.SemaphoreType.DMA((n_row,))
        named["leaving_recv%d" % c] = pltpu.SemaphoreType.DMA((n_row,))
    return named


def loop_factor(packed, count, work):
    lane = lax.broadcasted_iota(jnp.int32, (64, LANE), 1)
    line = lax.broadcasted_iota(jnp.int32, (64, LANE), 0)
    sub = lax.broadcasted_iota(jnp.int32, (8, LANE), 0)
    gram = jnp.concatenate([packed, pltpu.roll(packed, 64, 1)], axis=0) * (1.0 / count)
    work[...] = jnp.where(lane < 64, gram, jnp.where(lane - 64 == line, 1.0, 0.0))

    def eliminate(kb):
        base = pl.multiple_of(kb * 8, 8)
        shift = lax.rem(LANE - base, LANE)
        block = work[pl.ds(base, 8), :]
        whole = work[...]
        near = pltpu.roll(block, shift, 1)
        far = pltpu.roll(whole, shift, 1)
        heads = [jnp.broadcast_to(near[:, i : i + 1], (8, LANE)) for i in range(8)]
        cols = [jnp.broadcast_to(far[:, i : i + 1], (64, LANE)) for i in range(8)]
        lines = [jnp.broadcast_to(block[i : i + 1, :], (8, LANE)) for i in range(8)]
        diagonal = jnp.ones((8, LANE), f32)
        total = jnp.zeros((64, LANE), f32)
        final = lines[0]
        for i in range(8):
            pivot = jnp.broadcast_to(heads[i][i : i + 1, :], (8, LANE))
            diagonal = jnp.where(sub == i, pivot, diagonal)
            final = jnp.where(sub == i, lines[i], final)
            inverse = 1.0 / pivot
            scaled = lines[i] * inverse
            total = total + cols[i] * jnp.broadcast_to(scaled[:1], (64, LANE))
            for j in range(i + 1, 8):
                ratio = jnp.broadcast_to(heads[i][j : j + 1, :], (8, LANE)) * inverse
                lines[j] = lines[j] - ratio * lines[i]
                heads[j] = heads[j] - heads[i] * ratio
                cols[j] = cols[j] - cols[i] * jnp.broadcast_to(ratio[:1], (64, LANE))
        work[...] = whole - jnp.where(line >= base + 8, total, 0.0)
        work[pl.ds(base, 8), :] = final / jnp.sqrt(diagonal)

    loop(0, 8, eliminate)


def inverse_of(work):
    both = work[...]
    lane = lax.broadcasted_iota(jnp.int32, both.shape, 1)
    return jnp.where(lane < 64, pltpu.roll(both, 64, 1), 0.0)


def whole_kernel(sizes, chunks, totals, names, info_ref, tiles_ref, own_ref, ids_ref, *refs):
    n_row, n_col, nx = sizes
    total_rows, total_cols = totals
    held_ref, gram_ref, basis_ref = refs[:3]
    r = dict(zip(names, refs[3:]))
    row, col = lax.axis_index("row"), lax.axis_index("col")
    capacity = tiles_ref.shape[0]
    starts = {"owner": 0, "place": capacity, "before": 2 * capacity, "last": 3 * capacity}
    starts["slot"] = 3 * capacity + 2 * n_col
    info = {
        name: functools.partial(lambda first, i: info_ref[first + i], first)
        for name, first in starts.items()
    }
    splits = [r["high"], r["middle"], r["low"]]
    wanted = r["wanted"]
    width = own_ref.shape[0]
    rows = width // chunks
    columns_ref, work, held = r["columns"], r["work"], r["held"]

    greet(n_row, n_col, row, col, True, True)
    ids = Exchange(
        n_row,
        row,
        lambda p: ids_ref.at[p],
        wanted,
        r["id_send"],
        r["id_recv"],
        lambda p: (p, col),
    )
    ids.start()
    wanted[row] = ids_ref[row]

    def split(t):
        for ref, piece in zip(splits, three(tiles_ref[t])):
            ref[t] = piece

    loop(0, capacity, split)

    spread = Spread(n_row, row, col, chunks, r, "one_")
    sums = [RowSums(n_col, row, col, c, r, "one_") for c in range(chunks)]
    spread.start(own_ref, lambda peer: ids.copy_from(peer).wait())
    for c in range(chunks):
        spread.finish(c)
        sums[c].sketch(spread.got[c], splits, info)
        sums[c].start()
        sums[c].pair_up()
    for c in range(chunks):
        total = sums[c].total()
        sums[c].gather(total)
        held[:, c * rows : (c + 1) * rows] = total
    gram_one = GramSum(sizes, row, col, r, "gram_one_")
    gram_one.scatter_x(pack_gram(held[0]) + pack_gram(held[1]))
    moves = [ColumnSums(n_row, row, col, c, r) for c in range(chunks)]
    steps = [gram_one.sum_z, gram_one.sum_columns, gram_one.gather_x]
    for c in range(chunks):
        sums[c].gathered()
        if c + 1 == chunks:
            for step in steps[1:]:
                step()
        elif c == 0:
            steps[0]()
        moves[c].start(sums[c].group, splits, info)
    if chunks == 1:
        for step in steps:
            step()
    loop_factor(gram_one.result(), total_rows, work)
    inverse_one = inverse_of(work)
    for c in range(chunks):
        moves[c].finish(columns_ref, c * rows)

    def normalise(b, packed):
        block = apply_inverse(inverse_one, columns_ref[b])
        columns_ref[b] = block
        return packed + pack_gram(block)

    packed = lax.fori_loop(0, columns_ref.shape[0], normalise, jnp.zeros((32, LANE), f32))
    gram_cols = GramSum(sizes, row, col, r, "gram_cols_")
    gram_cols.scatter_x(packed)
    gram_cols.sum_z()
    gram_cols.sum_columns()
    gram_cols.gather_x()
    loop_factor(gram_cols.result(), total_cols, work)
    inverse_cols = inverse_of(work)
    for b in range(columns_ref.shape[0]):
        basis_ref[:, b * LANE : (b + 1) * LANE] = apply_inverse(inverse_cols, columns_ref[b]).astype(
            bf16
        )

    spread = Spread(n_row, row, col, chunks, r, "two_")
    sums = [RowSums(n_col, row, col, c, r, "two_") for c in range(chunks)]
    spread.start(basis_ref)
    for c in range(chunks):
        spread.finish(c)
        sums[c].sketch(spread.got[c], splits, info)
        sums[c].start()
        sums[c].pair_up()
    for c in range(chunks):
        held_ref[:, c * rows : (c + 1) * rows] = sums[c].total()
    gram_two = GramSum(sizes, row, col, r, "gram_two_")
    gram_two.scatter_x(pack_gram(held_ref[0]) + pack_gram(held_ref[1]))
    gram_two.sum_z()
    gram_two.sum_columns()
    gram_two.gather_x()
    gram_ref[...] = gram_two.result()


def whole_scratch(sizes, chunks, capacity, width, per_owner, block):
    n_row, n_col, nx = sizes
    named = {
        "wanted": pltpu.VMEM((n_row, 1, LANE), jnp.int32),
        "id_send": pltpu.SemaphoreType.DMA((n_row,)),
        "id_recv": pltpu.SemaphoreType.DMA((n_row,)),
        "high": pltpu.VMEM((capacity, block, block), bf16),
        "middle": pltpu.VMEM((capacity, block, block), bf16),
        "low": pltpu.VMEM((capacity, block, block), bf16),
        "columns": pltpu.VMEM((per_owner, width, LANE), f32),
        "held": pltpu.VMEM((2, width, LANE), f32),
        "work": pltpu.VMEM((width, LANE), f32),
    }
    for tag in ("gram_one_", "gram_cols_", "gram_two_"):
        named.update(gram_scratch(sizes, tag))
    named.update(spread_scratch(n_row, chunks, width, "one_"))
    named.update(spread_scratch(n_row, chunks, width, "two_"))
    named.update(row_scratch(n_col, capacity, chunks, width, "one_", True))
    named.update(row_scratch(n_col, capacity, chunks, width, "two_", False))
    named.update(column_scratch(n_row, capacity, chunks, width))
    return named


def factor(gram_ref, count):
    packed = gram_ref[...].reshape(32, LANE)
    lane = lax.broadcasted_iota(jnp.int32, (8, LANE), 1)
    sub = lax.broadcasted_iota(jnp.int32, (8, LANE), 0)
    turned = pltpu.roll(packed, 64, 1)
    groups = []
    for g in range(8):
        source = packed if g < 4 else turned
        h = g % 4
        left = source[h * 8 : (h + 1) * 8] * (1.0 / count)
        ident = jnp.where(lane - 64 == sub + g * 8, 1.0, 0.0).astype(f32)
        groups.append(jnp.where(lane < 64, left, ident))
    pivots = []
    for kb in range(8):
        below = range(kb, 8)
        cols = [
            {g: jnp.broadcast_to(groups[g][:, 8 * kb + i : 8 * kb + i + 1], (8, LANE)) for g in below}
            for i in range(8)
        ]
        lines = [jnp.broadcast_to(groups[kb][i : i + 1, :], (8, LANE)) for i in range(8)]
        scaled = []
        diagonal = jnp.ones((8, LANE), f32)
        for i in range(8):
            pivot = jnp.broadcast_to(cols[i][kb][i : i + 1, :], (8, LANE))
            diagonal = jnp.where(sub == i, pivot, diagonal)
            inverse = 1.0 / pivot
            scaled.append(lines[i] * inverse)
            for j in range(i + 1, 8):
                ratio = jnp.broadcast_to(cols[i][kb][j : j + 1, :], (8, LANE)) * inverse
                lines[j] = lines[j] - ratio * lines[i]
                for g in below:
                    cols[j][g] = cols[j][g] - cols[i][g] * ratio
        block = lines[0]
        for i in range(1, 8):
            block = jnp.where(sub == i, lines[i], block)
        groups[kb] = block
        pivots.append(diagonal)
        for g in range(kb + 1, 8):
            for i in range(8):
                groups[g] = groups[g] - cols[i][g] * scaled[i]
    return [groups[g] / jnp.sqrt(pivots[g]) for g in range(8)]


def split_factor(groups):
    both = jnp.concatenate(groups, axis=0)
    lane = lax.broadcasted_iota(jnp.int32, both.shape, 1)
    sub = lax.broadcasted_iota(jnp.int32, both.shape, 0)
    upper = jnp.where((lane < 64) & (lane >= sub), both, 0.0)
    inverse = jnp.where(lane < 64, pltpu.roll(both, 64, 1), 0.0)
    return upper, inverse


def apply_inverse(inverse, block):
    return nn(inverse, jnp.concatenate([block, jnp.zeros_like(block)], axis=0))


def final_kernel(count, gram_ref, held_ref, basis_ref, q_ref, w_ref, r_ref):
    upper, inverse = split_factor(factor(gram_ref, count))
    r_ref[...] = upper[:, :64]
    w_ref[...] = basis_ref[...]
    for b in range(held_ref.shape[0]):
        q_ref[:, b * LANE : (b + 1) * LANE] = apply_inverse(inverse, held_ref[b])


def call(body, outs, ins, scratch=(), smem=0, collective=None):
    vmem = pl.BlockSpec(memory_space=pltpu.VMEM)
    return pl.pallas_call(
        body,
        out_shape=[jax.ShapeDtypeStruct(shape, kind) for shape, kind in outs],
        in_specs=[pl.BlockSpec(memory_space=pltpu.SMEM)] * smem + [vmem] * (len(ins) - smem),
        out_specs=[vmem] * len(outs),
        scratch_shapes=list(scratch),
        compiler_params=pltpu.CompilerParams(
            collective_id=collective,
            has_side_effects=collective is not None,
            vmem_limit_bytes=24 * 1024 * 1024,
        ),
    )(*ins)


def shards(n_row, n_col, nx, tiles, coords, counts, probes):
    sizes = (n_row, n_col, nx)
    capacity, block = tiles.shape[0], tiles.shape[1]
    width, share = probes.shape[0], probes.shape[2]
    per_owner = share // block
    group_blocks = 2 * n_col
    total_rows = group_blocks * n_row * block
    total_cols = share * n_row * n_col
    order = jnp.arange(capacity, dtype=jnp.int32)
    live = order < counts[0]
    place = coords[:, 0] % group_blocks
    col_local = coords[:, 1] % (per_owner * n_row)
    owner = col_local // per_owner
    within = col_local % per_owner

    def latest(keys, wanted, allowed):
        match = (keys[:, None] == wanted[None, :]) & live[:, None] & allowed
        found = jnp.max(jnp.where(match, order[:, None], -1), axis=0)
        return jnp.where(found < 0, capacity, found)

    rows_wanted = jnp.arange(group_blocks, dtype=jnp.int32)
    owners = jnp.arange(n_row, dtype=jnp.int32)
    before = latest(place, place, order[:, None] < order[None, :])
    info = jnp.concatenate(
        [owner, place, before, latest(place, rows_wanted, True), latest(owner, owners, True)]
    ).astype(jnp.int32)
    match = (owner[:, None] == owners[None, :]) & live[:, None]
    ids = jnp.sum(jnp.where(match, within[:, None] + 1, 0), axis=0)
    ids = jnp.broadcast_to(ids[:, None, None], (n_row, 1, LANE)).astype(jnp.int32)

    scratch = whole_scratch(sizes, CHUNKS, capacity, width, per_owner, block)
    held, gram, basis = call(
        functools.partial(whole_kernel, sizes, CHUNKS, (total_rows, total_cols), list(scratch)),
        [((2, width, LANE), f32), ((32, LANE), f32), ((width, share), bf16)],
        (info, tiles, probes.reshape(width, share), ids),
        scratch.values(),
        smem=1,
        collective=0,
    )
    q_basis, w_basis, r_factor = call(
        functools.partial(final_kernel, total_rows),
        [((width, 2 * LANE), f32), ((width, share), bf16), ((width, width), f32)],
        (gram, held, basis),
    )
    return (q_basis, w_basis.reshape(width, 1, share), r_factor)


def solution(mesh):
    n_row, n_col = mesh.shape["row"], mesh.shape["col"]
    nx = 4 if n_row >= 16 else 2
    in_specs = (
        P(("row", "col"), None, None),
        P(("row", "col"), None),
        P(("row", "col")),
        P(None, "col", "row"),
    )
    out_specs = (P(None, ("row", "col")), P(None, "col", "row"), P())
    return jax.shard_map(
        functools.partial(shards, n_row, n_col, nx),
        mesh=mesh,
        in_specs=in_specs,
        out_specs=out_specs,
        check_vma=False,
    )
```

time: 752 us -> 164 us (0.22)
  waiting for transfers between devices: 344 us -> 0 us
  blocking collectives: 297 us -> 0 us
  Pallas kernels: 0 us -> 159 us
  other arithmetic: 39.9 us -> 0.25 us
  local copies, waits for them, and re-layouts: 27 us -> 2.97 us
  starting transfers between devices: 14.8 us -> 0 us
  matrix products: 14 us -> 0 us
  between operations: 14.7 us -> 1.35 us
    psum x3 -> x0, blocking collectives: 297 us -> none  [the longest x2 200 us: reduce_rows(): gram = lax.psum(product(held, held.T), ('row', 'col'))]
    all_gather x3 -> x0, waiting for transfers between devices: 202 us -> none  [the longest x2 172 us: fetch(): lax.all_gather(own, 'row', axis=1, tiled=True)]
    pallas_call x0 -> x2, Pallas kernels: none -> 159 us  [call(): pl.pallas_call(body, out_shape=[jax.ShapeDtypeStruct(shape, kind) for sha...]
    reduce_scatter x2 -> x0, waiting for transfers between devices: 115 us -> none  [reduce_rows(): lax.psum_scatter(partial_rows, 'col', scatter_dimension=1, tiled=True)]
    another operation x14 -> x0, other arithmetic: 35.6 us -> none  [the longest x5 16 us: lower_inverse(): return jax.scipy.linalg.solve_triangular(lower, ident, lower=True)]
    all_to_all x2 -> x0, waiting for transfers between devices: 26.2 us -> none  [the longest x1 26.2 us: shards(): lax.all_to_all(outgoing, 'row', split_axis=0, concat_axis=0, tiled=True)]
    all_to_all x2 -> x0, starting transfers between devices: 14.6 us -> none  [the longest x1 9.93 us: shards(): lax.all_to_all(outgoing, 'row', split_axis=0, concat_axis=0, tiled=True)]
    dot_general x12 -> x0, matrix products: 13.2 us -> none  [the longest x6 6.98 us: product(): jnp.dot(left, right, preferred_element_type=jnp.float32, precision=highest)]
  transfers between devices with their start and end apart: 7 -> 0, of which waited for: 6 -> 0; matrix products, arithmetic and copies ran while one was open for 1% -> 0% of each run, Pallas kernels for 0% -> 0%
where the time goes in v1:
time: 164 us
  Pallas kernels  159 us (97%)
  local copies, waits for them, and re-layouts  2.97 us (2%)
    pallas_call x2, Pallas kernels, call(): pl.pallas_call(body, out_shape=[jax.ShapeDtypeStruct(shape, kind) for sha...  159 us

profile of v1, /device:TPU:1, one launch (start us, length us, event | category | flops | bytes accessed | tf_op | source)
XLA Modules:
  0.0 164.0 jit_solution(10695961869623813088)
XLA Ops:
  1.3 0.0 copy-start.2
  1.3 0.7 copy-done.2
  2.0 0.1 select_reduce_fusion.3
  2.1 0.1 select_reduce_fusion
  2.2 0.1 concatenate.3.info_ref
  2.3 0.1 broadcast_in_dim.80.ids_ref
  2.4 0.0 copy-start
  2.4 1.2 copy-done
  3.6 0.0 copy-start.1
  3.7 0.9 copy-done.1
  4.6 156.8 %shard_map.67 = (f32[2,64,128]{2,1,0:T(8,128)S(1)}, f32[32,128]{1,0:T(8,128)S(1)}, bf16[64,1024]{1,0:T(8,128)(2,1)S(1)}) custom-call(s32[112]{0:T(128)S(1)} %concatenate.3.info_ref, f32[16,128,128]{2,1,0:T(8,128)S(1)} %copy-done, bf16[64,1024]{1,0:T(8,128)(2,1)S(1)} %bitcast.16, s32[32,1,128]{2,1,0:T(1,128)S(1)} %broadcast_in_dim.80.ids_ref), custom_call_target="tpu_custom_call" | custom-call | tf_op jit(solution)/shard_map/pallas_call | solution.py:738
  161.4 2.6 %shard_map.68 = (f32[64,256]{1,0:T(8,128)}, bf16[64,1024]{1,0:T(8,128)(2,1)}, f32[64,64]{1,0:T(8,128)}) custom-call(f32[32,128]{1,0:T(8,128)S(1)} %get-tuple-element.9.gram_ref, f32[2,64,128]{2,1,0:T(8,128)S(1)} %get-tuple-element.10.held_ref, bf16[64,1024]{1,0:T(8,128)(2,1)S(1)} %get-tuple-element.11.basis_ref), custom_call_target="tpu_custom_call" | custom-call | tf_op jit(solution)/shard_map/pallas_call | solution.py:738
  (6 shorter events, 0.1 us)
Async XLA Ops:
  1.3 0.7 copy-start.2
  2.4 1.2 copy-start
  3.6 0.9 copy-start.1

commit v2 on v1

--- a/solution.py
+++ b/solution.py
@@ -13,7 +13,8 @@
 bf16 = jnp.bfloat16
 LANE = 128
 CORES = 2
-CHUNKS = 2
+CHUNKS = 4
+TOGETHER = 4
 
 
 def nn(left, right):
@@ -313,12 +314,15 @@
     def sketch(self, got, splits, info):
         capacity = splits[0].shape[0]
         dims = (((1,), (1,)), ((), ()))
-        for t in range(capacity):
+
+        def multiply(t):
             block = got[info["owner"](t)]
             total = lax.dot_general(block, splits[2][t], dims, preferred_element_type=f32)
             total += lax.dot_general(block, splits[1][t], dims, preferred_element_type=f32)
             total += lax.dot_general(block, splits[0][t], dims, preferred_element_type=f32)
             self.terms[t] = total
+
+        each_tile(capacity, multiply)
         self.terms[capacity] = jnp.zeros(self.terms.shape[1:], f32)
 
         def chain(t):
@@ -414,6 +418,14 @@
     return named
 
 
+def each_tile(capacity, body):
+    def some(q):
+        for j in range(TOGETHER):
+            body(q * TOGETHER + j)
+
+    loop(0, capacity // TOGETHER, some)
+
+
 def three(value):
     high = value.astype(bf16)
     rest = value - high.astype(f32)
@@ -449,7 +461,7 @@
                 left, right, (((1,), (0,)), ((), ())), preferred_element_type=f32
             )
 
-        for t in range(capacity):
+        def multiply(t):
             place = info["place"](t)
             source = group[place // 2, lax.rem(place, 2)]
             high, middle, low = three(source)
@@ -458,6 +470,8 @@
             by_low = dot(high, splits[2][t])
             small = by_high[2 * rows :] + by_middle[rows:] + by_low
             self.terms[t] = by_high[:rows] + (by_high[rows : 2 * rows] + by_middle[:rows] + small)
+
+        each_tile(capacity, multiply)
         self.terms[capacity] = jnp.zeros(self.terms.shape[1:], f32)
 
         def serve(k):
@@ -540,12 +554,17 @@
     return jnp.where(lane < 64, pltpu.roll(both, 64, 1), 0.0)
 
 
-def whole_kernel(sizes, chunks, totals, names, info_ref, tiles_ref, own_ref, ids_ref, *refs):
+def whole_kernel(sizes, chunks, totals, names, info_ref, ids_ref, tiles_hbm, own_hbm, *refs):
     n_row, n_col, nx = sizes
     total_rows, total_cols = totals
     held_ref, gram_ref, basis_ref = refs[:3]
     r = dict(zip(names, refs[3:]))
     row, col = lax.axis_index("row"), lax.axis_index("col")
+    tiles_ref, own_ref = r["tiles"], r["own"]
+    load_own = pltpu.make_async_copy(own_hbm, own_ref, r["load_sem"].at[0])
+    load_tiles = pltpu.make_async_copy(tiles_hbm, tiles_ref, r["load_sem"].at[1])
+    load_own.start()
+    load_tiles.start()
     capacity = tiles_ref.shape[0]
     starts = {"owner": 0, "place": capacity, "before": 2 * capacity, "last": 3 * capacity}
     starts["slot"] = 3 * capacity + 2 * n_col
@@ -576,35 +595,42 @@
         for ref, piece in zip(splits, three(tiles_ref[t])):
             ref[t] = piece
 
-    loop(0, capacity, split)
-
     spread = Spread(n_row, row, col, chunks, r, "one_")
     sums = [RowSums(n_col, row, col, c, r, "one_") for c in range(chunks)]
+    load_own.wait()
     spread.start(own_ref, lambda peer: ids.copy_from(peer).wait())
+    load_tiles.wait()
+    loop(0, capacity, split)
+    gram_one = GramSum(sizes, row, col, r, "gram_one_")
+    moves = [ColumnSums(n_row, row, col, c, r) for c in range(chunks)]
+
+    def gather(c):
+        total = sums[c].total()
+        sums[c].gather(total)
+        held[:, c * rows : (c + 1) * rows] = total
+
+    def send_terms(c):
+        sums[c].gathered()
+        moves[c].start(sums[c].group, splits, info)
+
     for c in range(chunks):
         spread.finish(c)
         sums[c].sketch(spread.got[c], splits, info)
         sums[c].start()
+        if c >= 1:
+            gather(c - 1)
         sums[c].pair_up()
-    for c in range(chunks):
-        total = sums[c].total()
-        sums[c].gather(total)
-        held[:, c * rows : (c + 1) * rows] = total
-    gram_one = GramSum(sizes, row, col, r, "gram_one_")
+        if c >= 2:
+            send_terms(c - 2)
+    gather(chunks - 1)
     gram_one.scatter_x(pack_gram(held[0]) + pack_gram(held[1]))
-    moves = [ColumnSums(n_row, row, col, c, r) for c in range(chunks)]
-    steps = [gram_one.sum_z, gram_one.sum_columns, gram_one.gather_x]
-    for c in range(chunks):
-        sums[c].gathered()
-        if c + 1 == chunks:
-            for step in steps[1:]:
-                step()
-        elif c == 0:
-            steps[0]()
-        moves[c].start(sums[c].group, splits, info)
-    if chunks == 1:
-        for step in steps:
-            step()
+    if chunks >= 2:
+        send_terms(chunks - 2)
+    gram_one.sum_z()
+    sums[chunks - 1].gathered()
+    gram_one.sum_columns()
+    moves[chunks - 1].start(sums[chunks - 1].group, splits, info)
+    gram_one.gather_x()
     loop_factor(gram_one.result(), total_rows, work)
     inverse_one = inverse_of(work)
     for c in range(chunks):
@@ -631,13 +657,19 @@
     spread = Spread(n_row, row, col, chunks, r, "two_")
     sums = [RowSums(n_col, row, col, c, r, "two_") for c in range(chunks)]
     spread.start(basis_ref)
+
+    def keep(c):
+        held_ref[:, c * rows : (c + 1) * rows] = sums[c].total()
+
     for c in range(chunks):
         spread.finish(c)
         sums[c].sketch(spread.got[c], splits, info)
         sums[c].start()
+        if c >= 2:
+            keep(c - 2)
         sums[c].pair_up()
-    for c in range(chunks):
-        held_ref[:, c * rows : (c + 1) * rows] = sums[c].total()
+    for c in range(max(chunks - 2, 0), chunks):
+        keep(c)
     gram_two = GramSum(sizes, row, col, r, "gram_two_")
     gram_two.scatter_x(pack_gram(held_ref[0]) + pack_gram(held_ref[1]))
     gram_two.sum_z()
@@ -649,6 +681,9 @@
 def whole_scratch(sizes, chunks, capacity, width, per_owner, block):
     n_row, n_col, nx = sizes
     named = {
+        "tiles": pltpu.VMEM((capacity, block, block), f32),
+        "own": pltpu.VMEM((width, per_owner * block), bf16),
+        "load_sem": pltpu.SemaphoreType.DMA((2,)),
         "wanted": pltpu.VMEM((n_row, 1, LANE), jnp.int32),
         "id_send": pltpu.SemaphoreType.DMA((n_row,)),
         "id_recv": pltpu.SemaphoreType.DMA((n_row,)),
@@ -733,18 +768,20 @@
         q_ref[:, b * LANE : (b + 1) * LANE] = apply_inverse(inverse, held_ref[b])
 
 
-def call(body, outs, ins, scratch=(), smem=0, collective=None):
+def call(body, outs, ins, scratch=(), smem=0, anywhere=0, collective=None):
     vmem = pl.BlockSpec(memory_space=pltpu.VMEM)
     return pl.pallas_call(
         body,
         out_shape=[jax.ShapeDtypeStruct(shape, kind) for shape, kind in outs],
-        in_specs=[pl.BlockSpec(memory_space=pltpu.SMEM)] * smem + [vmem] * (len(ins) - smem),
+        in_specs=[pl.BlockSpec(memory_space=pltpu.SMEM)] * smem
+        + [vmem] * (len(ins) - smem - anywhere)
+        + [pl.BlockSpec(memory_space=pl.ANY)] * anywhere,
         out_specs=[vmem] * len(outs),
         scratch_shapes=list(scratch),
         compiler_params=pltpu.CompilerParams(
             collective_id=collective,
             has_side_effects=collective is not None,
-            vmem_limit_bytes=24 * 1024 * 1024,
+            vmem_limit_bytes=62 * 1024 * 1024,
         ),
     )(*ins)
 
@@ -783,9 +820,10 @@
     held, gram, basis = call(
         functools.partial(whole_kernel, sizes, CHUNKS, (total_rows, total_cols), list(scratch)),
         [((2, width, LANE), f32), ((32, LANE), f32), ((width, share), bf16)],
-        (info, tiles, probes.reshape(width, share), ids),
+        (info, ids, tiles, probes.reshape(width, share)),
         scratch.values(),
         smem=1,
+        anywhere=2,
         collective=0,
     )
     q_basis, w_basis, r_factor = call(

time: 164 us -> 185 us (1.13)
  Pallas kernels: 159 us -> 181 us
    pallas_call x2, Pallas kernels: 159 us -> 181 us  [call(): pl.pallas_call(body, out_shape=[jax.ShapeDtypeStruct(shape, kind) for sha...]
    unnamed x6 -> x2, local copies, waits for them, and re-layouts: 2.8 us -> 0.67 us
where the time goes in v2:
time: 185 us
  Pallas kernels  181 us (98%)
  local copies, waits for them, and re-layouts  1.97 us (1%)
    pallas_call x2, Pallas kernels, call(): pl.pallas_call(body, out_shape=[jax.ShapeDtypeStruct(shape, kind) for sha...  181 us

profile of v2, /device:TPU:1, one launch (start us, length us, event | category | flops | bytes accessed | tf_op | source)
XLA Modules:
  0.0 184.8 jit_solution(18341304930439341171)
XLA Ops:
  1.3 0.0 copy-start
  1.3 0.7 copy-done
  2.0 0.1 select_reduce_fusion.3
  2.1 0.1 select_reduce_fusion
  2.2 0.6 concatenate.3.info_ref
  2.8 0.7 broadcast_in_dim.80.ids_ref
  3.5 177.6 %shard_map.67 = (f32[2,64,128]{2,1,0:T(8,128)}, f32[32,128]{1,0:T(8,128)}, bf16[64,1024]{1,0:T(8,128)(2,1)}) custom-call(s32[112]{0:T(128)} %concatenate.3.info_ref, s32[32,1,128]{2,1,0:T(1,128)} %broadcast_in_dim.80.ids_ref, f32[16,128,128]{2,1,0:T(8,128)} %tiles_hbm.1, bf16[64,1024]{1,0:T(8,128)(2,1)} %bitcast.16), custom_call_target="tpu_custom_call" | custom-call | tf_op jit(solution)/shard_map/pallas_call | solution.py:773
  181.2 3.6 %shard_map.68 = (f32[64,256]{1,0:T(8,128)}, bf16[64,1024]{1,0:T(8,128)(2,1)}, f32[64,64]{1,0:T(8,128)}) custom-call(f32[32,128]{1,0:T(8,128)} %get-tuple-element.9.gram_ref, f32[2,64,128]{2,1,0:T(8,128)} %get-tuple-element.10.held_ref, bf16[64,1024]{1,0:T(8,128)(2,1)} %get-tuple-element.11.basis_ref), custom_call_target="tpu_custom_call" | custom-call | tf_op jit(solution)/shard_map/pallas_call | solution.py:773
  (6 shorter events, 0.1 us)
Async XLA Ops:
  1.3 0.7 copy-start

commit v3 on v2

--- a/solution.py
+++ b/solution.py
@@ -13,8 +13,8 @@
 bf16 = jnp.bfloat16
 LANE = 128
 CORES = 2
-CHUNKS = 4
-TOGETHER = 4
+CHUNKS = 2
+TOGETHER = 8
 
 
 def nn(left, right):
@@ -53,28 +53,19 @@
     return n // 2 + step * (2 * lax.rem(k, 2) - 1)
 
 
-def greet(n_row, n_col, row, col, with_row, with_col):
+def greet(sizes, row, col):
+    n_row, n_col, nx = sizes
+    nz = n_row // nx
+    z, x = row // nx, lax.rem(row, nx)
     barrier = pltpu.get_barrier_semaphore()
-    count = 0
-    if with_row:
-        loop(
-            1,
-            n_row,
-            lambda d: pl.semaphore_signal(
-                barrier, inc=1, device_id=(lax.rem(row + d, n_row), col), device_id_type=MESH
-            ),
-        )
-        count += n_row - 1
-    if with_col:
-        loop(
-            1,
-            n_col,
-            lambda d: pl.semaphore_signal(
-                barrier, inc=1, device_id=(row, lax.rem(col + d, n_col)), device_id_type=MESH
-            ),
-        )
-        count += n_col - 1
-    pl.semaphore_wait(barrier, count)
+
+    def signal(device):
+        pl.semaphore_signal(barrier, inc=1, device_id=device, device_id_type=MESH)
+
+    loop(1, nx, lambda d: signal((z * nx + lax.rem(x + d, nx), col)))
+    loop(1, nz, lambda d: signal((lax.rem(z + d, nz) * nx + x, col)))
+    loop(1, n_col, lambda d: signal((row, lax.rem(col + d, n_col))))
+    pl.semaphore_wait(barrier, nx + nz + n_col - 3)
 
 
 class Exchange:
@@ -82,35 +73,19 @@
         self.n, self.me, self.source, self.dst = n, me, source, dst
         self.send, self.recv, self.device = send, recv, device
 
-    def copy_to(self, peer):
-        return remote(
-            self.source(peer),
-            self.dst.at[self.me],
-            self.send.at[peer],
-            self.recv.at[self.me],
-            self.device(peer),
-        )
-
-    def copy_from(self, peer):
-        return remote(
-            self.source(peer),
-            self.dst.at[peer],
-            self.send.at[peer],
-            self.recv.at[peer],
-            self.device(peer),
-        )
+    def start_one(self, k):
+        peer = lax.rem(self.me + offset(k, self.n), self.n)
+        remote(
+            self.source(peer), self.dst.at[self.me], self.send, self.recv, self.device(peer)
+        ).start()
 
     def start(self):
-        loop(
-            0, self.n - 1, lambda k: self.copy_to(lax.rem(self.me + offset(k, self.n), self.n)).start()
-        )
+        loop(0, self.n - 1, self.start_one)
 
     def wait(self):
-        loop(
-            0,
-            self.n - 1,
-            lambda k: self.copy_from(lax.rem(self.me - offset(k, self.n) + self.n, self.n)).wait(),
-        )
+        everything = self.dst.at[pl.ds(0, self.n - 1)]
+        device = self.device(lax.rem(self.me + 1, self.n))
+        remote(everything, everything, self.send, self.recv, device).wait()
 
 
 def sum_slots(ref, n):
@@ -195,14 +170,14 @@
         "s2": pltpu.VMEM((depth, LANE), f32),
         "gc": pltpu.VMEM((n_col, depth, LANE), f32),
         "out": pltpu.VMEM((nx, depth, LANE), f32),
-        "x_send": dma((nx,)),
-        "x_recv": dma((nx,)),
-        "z_send": dma((nz,)),
-        "z_recv": dma((nz,)),
-        "c_send": dma((n_col,)),
-        "c_recv": dma((n_col,)),
-        "o_send": dma((nx,)),
-        "o_recv": dma((nx,)),
+        "x_send": dma,
+        "x_recv": dma,
+        "z_send": dma,
+        "z_recv": dma,
+        "c_send": dma,
+        "c_recv": dma,
+        "o_send": dma,
+        "o_recv": dma,
     }
     return {tag + name: shape for name, shape in named.items()}
 
@@ -215,72 +190,120 @@
     return total.astype(bf16)
 
 
+class RowExchange:
+    def __init__(self, sizes, row, col, out, r, tag):
+        n_row, n_col, nx = sizes
+        nz = n_row // nx
+        z, x = row // nx, lax.rem(row, nx)
+        self.nx, self.nz, self.x, self.z, self.out = nx, nz, x, z, out
+        self.mid, self.got = r[tag + "mid"], r[tag + "got"]
+        self.along_x = Exchange(
+            nx,
+            x,
+            lambda p: out.at[p],
+            None,
+            r[tag + "x_send"],
+            r[tag + "x_recv"],
+            lambda p: (z * nx + p, col),
+        )
+        self.along_z = Exchange(
+            nz,
+            z,
+            lambda p: self.mid.at[p],
+            self.got,
+            r[tag + "z_send"],
+            r[tag + "z_recv"],
+            lambda p: (p * nx + x, col),
+        )
+
+    def x_peer(self, k):
+        return lax.rem(self.x + offset(k, self.nx), self.nx)
+
+    def send_x(self, k):
+        e = self.along_x
+        peer = self.x_peer(k)
+        remote(
+            self.out.at[peer], self.mid.at[:, self.x], e.send, e.recv, e.device(peer)
+        ).start()
+
+    def turn(self):
+        e = self.along_x
+        everything = self.out.at[pl.ds(0, self.nx - 1)]
+        remote(everything, everything, e.send, e.recv, e.device(self.x_peer(0))).wait()
+        self.along_z.start()
+        self.got[self.z] = self.mid[self.z]
+
+    def wait(self):
+        self.along_z.wait()
+
+
+def exchange_scratch(sizes, tag, shape, kind, out=True):
+    n_row, n_col, nx = sizes
+    nz = n_row // nx
+    named = {
+        tag + "mid": pltpu.VMEM((nz, nx) + shape, kind),
+        tag + "got": pltpu.VMEM((nz, nx) + shape, kind),
+    }
+    if out:
+        named[tag + "out"] = pltpu.VMEM((nx, nz) + shape, kind)
+    for name in ("x_send", "x_recv", "z_send", "z_recv"):
+        named[tag + name] = pltpu.SemaphoreType.DMA
+    return named
+
+
 class Spread:
-    def __init__(self, n_row, row, col, chunks, r, tag):
-        self.n_row, self.row, self.chunks = n_row, row, chunks
-        self.wanted = r["wanted"]
-        self.outgoing = [r[tag + "outgoing%d" % c] for c in range(chunks)]
-        self.got = [r[tag + "got%d" % c] for c in range(chunks)]
-        self.moves = [
-            Exchange(
-                n_row,
-                row,
-                functools.partial(lambda ref, p: ref.at[p], self.outgoing[c]),
-                self.got[c],
-                r[tag + "send%d" % c],
-                r[tag + "recv%d" % c],
-                lambda p: (p, col),
-            )
-            for c in range(chunks)
-        ]
-
-    def store(self, refs, place, block):
-        rows = block.shape[0] // self.chunks
+    def __init__(self, sizes, row, col, chunks, r, tag):
+        tags = [tag + "%d" % c for c in range(chunks)]
+        self.chunks, self.wanted = chunks, r["wanted_got"]
+        self.moves = [RowExchange(sizes, row, col, r[t + "out"], r, t) for t in tags]
+        self.got = [move.got for move in self.moves]
+
+    def start(self, own_ref):
+        first = self.moves[0]
+        rows = own_ref.shape[0] // self.chunks
+
+        def column(peer, store):
+            def one(p):
+                block = pick(own_ref[...], self.wanted[p, peer])
+                for c in range(self.chunks):
+                    store(self.moves[c], p, block[c * rows : (c + 1) * rows])
+
+            loop(0, first.nz, one)
+
+        def away(k):
+            peer = first.x_peer(k)
+
+            def store(move, p, block):
+                move.out[peer, p] = block
+
+            column(peer, store)
+            first.send_x(k)
+
+        def here(move, p, block):
+            move.mid[p, move.x] = block
+
+        loop(0, first.nx - 1, away)
+        column(first.x, here)
         for c in range(self.chunks):
-            refs[c][place] = block[c * rows : (c + 1) * rows]
-
-    def start(self, own_ref, ready=None):
-        def serve(k):
-            peer = lax.rem(self.row - offset(k, self.n_row) + self.n_row, self.n_row)
-            if ready is not None:
-                ready(peer)
-            self.store(self.outgoing, peer, pick(own_ref[...], self.wanted[peer]))
-            self.moves[0].copy_to(peer).start()
-
-        loop(0, self.n_row - 1, serve)
-        self.store(self.got, self.row, pick(own_ref[...], self.wanted[self.row]))
-
-    def finish(self, c):
-        def step(k):
-            peer = lax.rem(self.row - offset(k, self.n_row) + self.n_row, self.n_row)
-            self.moves[c].copy_from(peer).wait()
-            if c + 1 < self.chunks:
-                self.moves[c + 1].copy_to(peer).start()
-
-        loop(0, self.n_row - 1, step)
-
-
-def spread_scratch(n_row, chunks, width, tag):
-    rows = width // chunks
-    named = {}
-    for c in range(chunks):
-        named[tag + "outgoing%d" % c] = pltpu.VMEM((n_row, rows, LANE), bf16)
-        named[tag + "got%d" % c] = pltpu.VMEM((n_row, rows, LANE), bf16)
-        named[tag + "send%d" % c] = pltpu.SemaphoreType.DMA((n_row,))
-        named[tag + "recv%d" % c] = pltpu.SemaphoreType.DMA((n_row,))
-    return named
+            if c:
+                loop(0, first.nx - 1, self.moves[c].send_x)
+        for c in range(self.chunks):
+            self.moves[c].turn()
 
 
 class RowSums:
     def __init__(self, n_col, row, col, c, r, tag):
         self.ny = ny = n_col // CORES
-        self.n_col = n_col
         self.y, self.core = col // CORES, lax.rem(col, CORES)
-        self.row, self.col = row, col
-        self.other = col + 1 - 2 * self.core
+        self.row = row
+        core = self.core
+        self.other = (row, col + 1 - 2 * core)
         get = lambda name: r[tag + name + "%d" % c]
+        same_core = lambda p: (row, p * CORES + core)
         self.terms, self.part, self.near = get("contrib"), get("rows"), get("near")
-        self.near_send, self.near_recv = get("near_send"), get("near_recv")
+        self.near_move = remote(
+            self.part.at[1 - core], self.near, get("near_send"), get("near_recv"), self.other
+        )
         self.summed, self.far = get("summed"), get("far")
         self.shares = Exchange(
             ny,
@@ -289,34 +312,30 @@
             self.far,
             get("far_send"),
             get("far_recv"),
-            self.same_core,
+            same_core,
         )
         if tag + "group%d" % c in r:
             self.group = get("group")
-            self.all_send, self.all_recv = get("all_send"), get("all_recv")
-            self.pass_send, self.pass_recv = get("pass_send"), get("pass_recv")
-
-    def same_core(self, p):
-        return (self.row, p * CORES + self.core)
-
-    def near_copy(self, t):
-        return remote(
-            self.part.at[t * CORES + (1 - self.core)],
-            self.near.at[t],
-            self.near_send.at[t],
-            self.near_recv.at[t],
-            (self.row, self.other),
-        )
-
-    def peer(self, k):
-        return lax.rem(self.y + offset(k, self.ny), self.ny)
+            mine = self.group.at[core]
+            self.all_move = Exchange(
+                ny,
+                self.y,
+                lambda p: mine.at[self.y],
+                mine,
+                get("all_send"),
+                get("all_recv"),
+                same_core,
+            )
+            self.pass_move = remote(mine, mine, get("pass_send"), get("pass_recv"), self.other)
 
     def sketch(self, got, splits, info):
         capacity = splits[0].shape[0]
         dims = (((1,), (1,)), ((), ()))
+        nx = got.shape[1]
 
         def multiply(t):
-            block = got[info["owner"](t)]
+            owner = info["owner"](t)
+            block = got[owner // nx, lax.rem(owner, nx)]
             total = lax.dot_general(block, splits[2][t], dims, preferred_element_type=f32)
             total += lax.dot_general(block, splits[1][t], dims, preferred_element_type=f32)
             total += lax.dot_general(block, splits[0][t], dims, preferred_element_type=f32)
@@ -331,99 +350,69 @@
         loop(0, capacity, chain)
 
         def place(p):
-            for j in range(2):
-                self.part[p, j] = self.terms[info["last"](2 * p + j)]
-
-        loop(0, self.n_col, place)
-
-    def start(self):
-        loop(0, self.ny - 1, lambda k: self.near_copy(self.peer(k)).start())
-        self.near_copy(self.y).start()
+            for core in range(CORES):
+                for j in range(2):
+                    self.part[core, p, j] = self.terms[info["last"](2 * (CORES * p + core) + j)]
+
+        loop(0, self.ny, place)
+        self.near_move.start()
 
     def pair_up(self):
+        self.near_move.wait()
+
         def step(k):
-            peer = self.peer(k)
-            self.near_copy(peer).wait()
-            self.summed[peer] = self.part[peer * CORES + self.core] + self.near[peer]
-            self.shares.copy_to(peer).start()
+            peer = lax.rem(self.y + offset(k, self.ny), self.ny)
+            self.summed[peer] = self.part[self.core, peer] + self.near[peer]
+            self.shares.start_one(k)
 
         loop(0, self.ny - 1, step)
-        self.near_copy(self.y).wait()
-        self.far[self.y] = self.part[self.y * CORES + self.core] + self.near[self.y]
+        self.far[self.y] = self.part[self.core, self.y] + self.near[self.y]
 
     def total(self):
         self.shares.wait()
         return sum_slots(self.far, self.ny)
 
-    def pass_copy(self, slot, peer):
-        return remote(
-            self.group.at[slot],
-            self.group.at[slot],
-            self.pass_send.at[peer],
-            self.pass_recv.at[peer],
-            (self.row, self.other),
-        )
-
     def gather(self, total):
-        self.group[self.col] = total
-        mine = self.group.at[self.col]
-
-        def send(k):
-            peer = self.peer(k)
-            remote(
-                mine, mine, self.all_send.at[peer], self.all_recv.at[self.y], self.same_core(peer)
-            ).start()
-
-        loop(0, self.ny - 1, send)
-        self.pass_copy(self.col, self.y).start()
+        self.group[self.core, self.y] = total
+        self.all_move.start()
 
     def gathered(self):
-        def relay(k):
-            peer = lax.rem(self.y - offset(k, self.ny) + self.ny, self.ny)
-            slot = peer * CORES + self.core
-            remote(
-                self.group.at[self.col],
-                self.group.at[slot],
-                self.all_send.at[peer],
-                self.all_recv.at[peer],
-                self.same_core(peer),
-            ).wait()
-            self.pass_copy(slot, peer).start()
-
-        loop(0, self.ny - 1, relay)
-        loop(0, self.ny, lambda p: self.pass_copy(p * CORES + (1 - self.core), p).wait())
+        self.all_move.wait()
+        self.pass_move.start()
+        self.pass_move.wait()
 
 
 def row_scratch(n_col, capacity, chunks, width, tag, gather):
     ny = n_col // CORES
     rows = width // chunks
-    dma = pltpu.SemaphoreType.DMA
     named = {}
     for c in range(chunks):
         some = {
             "contrib": pltpu.VMEM((capacity + 1, rows, LANE), f32),
-            "rows": pltpu.VMEM((n_col, 2, rows, LANE), f32),
+            "rows": pltpu.VMEM((CORES, ny, 2, rows, LANE), f32),
             "near": pltpu.VMEM((ny, 2, rows, LANE), f32),
             "summed": pltpu.VMEM((ny, 2, rows, LANE), f32),
             "far": pltpu.VMEM((ny, 2, rows, LANE), f32),
         }
         sems = ["near_send", "near_recv", "far_send", "far_recv"]
         if gather:
-            some["group"] = pltpu.VMEM((n_col, 2, rows, LANE), f32)
+            some["group"] = pltpu.VMEM((CORES, ny, 2, rows, LANE), f32)
             sems += ["all_send", "all_recv", "pass_send", "pass_recv"]
         for name in sems:
-            some[name] = dma((ny,))
+            some[name] = pltpu.SemaphoreType.DMA
         for name, shape in some.items():
             named[tag + name + "%d" % c] = shape
     return named
 
 
 def each_tile(capacity, body):
+    together = min(TOGETHER, capacity)
+
     def some(q):
-        for j in range(TOGETHER):
-            body(q * TOGETHER + j)
-
-    loop(0, capacity // TOGETHER, some)
+        for j in range(together):
+            body(q * together + j)
+
+    loop(0, capacity // together, some)
 
 
 def three(value):
@@ -434,27 +423,14 @@
 
 
 class ColumnSums:
-    def __init__(self, n_row, row, col, c, r):
-        self.n_row, self.row = n_row, row
-        self.terms, self.outgoing, self.arrived = (
-            r["terms%d" % c],
-            r["leaving%d" % c],
-            r["arrived%d" % c],
-        )
-        self.wanted = r["wanted"]
-        self.moved = Exchange(
-            n_row,
-            row,
-            lambda p: self.outgoing.at[p],
-            self.arrived,
-            r["leaving_send%d" % c],
-            r["leaving_recv%d" % c],
-            lambda p: (p, col),
-        )
+    def __init__(self, sizes, row, col, c, r):
+        self.terms, self.wanted = r["terms%d" % c], r["wanted_got"]
+        self.move = RowExchange(sizes, row, col, r["sum%dout" % c], r, "sum%d" % c)
 
     def start(self, group, splits, info):
         capacity = splits[0].shape[0]
         rows = self.terms.shape[1]
+        move = self.move
 
         def dot(left, right):
             return lax.dot_general(
@@ -463,7 +439,9 @@
 
         def multiply(t):
             place = info["place"](t)
-            source = group[place // 2, lax.rem(place, 2)]
+            source = group[
+                lax.rem(place // 2, CORES), place // (2 * CORES), lax.rem(place, 2)
+            ]
             high, middle, low = three(source)
             by_high = dot(jnp.concatenate([high, middle, low], axis=0), splits[0][t])
             by_middle = dot(jnp.concatenate([high, middle], axis=0), splits[1][t])
@@ -474,40 +452,38 @@
         each_tile(capacity, multiply)
         self.terms[capacity] = jnp.zeros(self.terms.shape[1:], f32)
 
-        def serve(k):
-            peer = lax.rem(self.row + offset(k, self.n_row), self.n_row)
-            self.outgoing[peer] = self.terms[info["slot"](peer)]
-            self.moved.copy_to(peer).start()
-
-        loop(0, self.n_row - 1, serve)
-        self.arrived[self.row] = self.terms[info["slot"](self.row)]
+        def away(k):
+            peer = move.x_peer(k)
+
+            def one(p):
+                move.out[peer, p] = self.terms[info["slot"](p * move.nx + peer)]
+
+            loop(0, move.nz, one)
+            move.send_x(k)
+
+        def here(p):
+            move.mid[p, move.x] = self.terms[info["slot"](p * move.nx + move.x)]
+
+        loop(0, move.nx - 1, away)
+        loop(0, move.nz, here)
 
     def finish(self, columns_ref, first):
-        self.moved.wait()
-        rows = self.arrived.shape[1]
+        move = self.move
+        move.wait()
+        rows = self.terms.shape[1]
 
         def column(b):
-            def add(s, total):
-                hit = jnp.broadcast_to(self.wanted[s], (rows, LANE)) == b + 1
-                return total + jnp.where(hit, self.arrived[s], 0.0)
+            def add(p, total):
+                for q in range(move.nx):
+                    hit = jnp.broadcast_to(self.wanted[p, q], (rows, LANE)) == b + 1
+                    total = total + jnp.where(hit, move.got[p, q], 0.0)
+                return total
 
             columns_ref[b, first : first + rows] = lax.fori_loop(
-                0, self.n_row, add, jnp.zeros((rows, LANE), f32)
+                0, move.nz, add, jnp.zeros((rows, LANE), f32)
             )
 
         loop(0, columns_ref.shape[0], column)
-
-
-def column_scratch(n_row, capacity, chunks, width):
-    rows = width // chunks
-    named = {}
-    for c in range(chunks):
-        named["terms%d" % c] = pltpu.VMEM((capacity + 1, rows, LANE), f32)
-        named["leaving%d" % c] = pltpu.VMEM((n_row, rows, LANE), f32)
-        named["arrived%d" % c] = pltpu.VMEM((n_row, rows, LANE), f32)
-        named["leaving_send%d" % c] = pltpu.SemaphoreType.DMA((n_row,))
-        named["leaving_recv%d" % c] = pltpu.SemaphoreType.DMA((n_row,))
-    return named
 
 
 def loop_factor(packed, count, work):
@@ -573,36 +549,33 @@
         for name, first in starts.items()
     }
     splits = [r["high"], r["middle"], r["low"]]
-    wanted = r["wanted"]
     width = own_ref.shape[0]
     rows = width // chunks
     columns_ref, work, held = r["columns"], r["work"], r["held"]
 
-    greet(n_row, n_col, row, col, True, True)
-    ids = Exchange(
-        n_row,
-        row,
-        lambda p: ids_ref.at[p],
-        wanted,
-        r["id_send"],
-        r["id_recv"],
-        lambda p: (p, col),
-    )
-    ids.start()
-    wanted[row] = ids_ref[row]
+    greet(sizes, row, col)
+    ids = RowExchange(sizes, row, col, ids_ref, r, "wanted_")
+    loop(0, nx - 1, ids.send_x)
+
+    def own_id(p):
+        ids.mid[p, ids.x] = ids_ref[ids.x, p]
+
+    loop(0, ids.nz, own_id)
+    ids.turn()
 
     def split(t):
         for ref, piece in zip(splits, three(tiles_ref[t])):
             ref[t] = piece
 
-    spread = Spread(n_row, row, col, chunks, r, "one_")
+    spread = Spread(sizes, row, col, chunks, r, "one_")
     sums = [RowSums(n_col, row, col, c, r, "one_") for c in range(chunks)]
     load_own.wait()
-    spread.start(own_ref, lambda peer: ids.copy_from(peer).wait())
+    ids.wait()
+    spread.start(own_ref)
     load_tiles.wait()
     loop(0, capacity, split)
     gram_one = GramSum(sizes, row, col, r, "gram_one_")
-    moves = [ColumnSums(n_row, row, col, c, r) for c in range(chunks)]
+    moves = [ColumnSums(sizes, row, col, c, r) for c in range(chunks)]
 
     def gather(c):
         total = sums[c].total()
@@ -614,23 +587,27 @@
         moves[c].start(sums[c].group, splits, info)
 
     for c in range(chunks):
-        spread.finish(c)
+        spread.moves[c].wait()
         sums[c].sketch(spread.got[c], splits, info)
-        sums[c].start()
         if c >= 1:
             gather(c - 1)
         sums[c].pair_up()
         if c >= 2:
             send_terms(c - 2)
-    gather(chunks - 1)
+            moves[c - 2].move.turn()
+    last = chunks - 1
+    if last >= 1:
+        send_terms(last - 1)
+    gather(last)
+    if last >= 1:
+        moves[last - 1].move.turn()
     gram_one.scatter_x(pack_gram(held[0]) + pack_gram(held[1]))
-    if chunks >= 2:
-        send_terms(chunks - 2)
     gram_one.sum_z()
-    sums[chunks - 1].gathered()
+    sums[last].gathered()
     gram_one.sum_columns()
-    moves[chunks - 1].start(sums[chunks - 1].group, splits, info)
+    moves[last].start(sums[last].group, splits, info)
     gram_one.gather_x()
+    moves[last].move.turn()
     loop_factor(gram_one.result(), total_rows, work)
     inverse_one = inverse_of(work)
     for c in range(chunks):
@@ -654,7 +631,7 @@
             bf16
         )
 
-    spread = Spread(n_row, row, col, chunks, r, "two_")
+    spread = Spread(sizes, row, col, chunks, r, "two_")
     sums = [RowSums(n_col, row, col, c, r, "two_") for c in range(chunks)]
     spread.start(basis_ref)
 
@@ -662,9 +639,8 @@
         held_ref[:, c * rows : (c + 1) * rows] = sums[c].total()
 
     for c in range(chunks):
-        spread.finish(c)
+        spread.moves[c].wait()
         sums[c].sketch(spread.got[c], splits, info)
-        sums[c].start()
         if c >= 2:
             keep(c - 2)
         sums[c].pair_up()
@@ -684,9 +660,6 @@
         "tiles": pltpu.VMEM((capacity, block, block), f32),
         "own": pltpu.VMEM((width, per_owner * block), bf16),
         "load_sem": pltpu.SemaphoreType.DMA((2,)),
-        "wanted": pltpu.VMEM((n_row, 1, LANE), jnp.int32),
-        "id_send": pltpu.SemaphoreType.DMA((n_row,)),
-        "id_recv": pltpu.SemaphoreType.DMA((n_row,)),
         "high": pltpu.VMEM((capacity, block, block), bf16),
         "middle": pltpu.VMEM((capacity, block, block), bf16),
         "low": pltpu.VMEM((capacity, block, block), bf16),
@@ -696,11 +669,14 @@
     }
     for tag in ("gram_one_", "gram_cols_", "gram_two_"):
         named.update(gram_scratch(sizes, tag))
-    named.update(spread_scratch(n_row, chunks, width, "one_"))
-    named.update(spread_scratch(n_row, chunks, width, "two_"))
+    named.update(exchange_scratch(sizes, "wanted_", (1, LANE), jnp.int32, out=False))
+    rows = width // chunks
+    for c in range(chunks):
+        for tag, kind in (("one_", bf16), ("two_", bf16), ("sum", f32)):
+            named.update(exchange_scratch(sizes, tag + "%d" % c, (rows, LANE), kind))
+        named["terms%d" % c] = pltpu.VMEM((capacity + 1, rows, LANE), f32)
     named.update(row_scratch(n_col, capacity, chunks, width, "one_", True))
     named.update(row_scratch(n_col, capacity, chunks, width, "two_", False))
-    named.update(column_scratch(n_row, capacity, chunks, width))
     return named
 
 
@@ -814,7 +790,8 @@
     ).astype(jnp.int32)
     match = (owner[:, None] == owners[None, :]) & live[:, None]
     ids = jnp.sum(jnp.where(match, within[:, None] + 1, 0), axis=0)
-    ids = jnp.broadcast_to(ids[:, None, None], (n_row, 1, LANE)).astype(jnp.int32)
+    ids = ids.reshape(n_row // nx, nx).T
+    ids = jnp.broadcast_to(ids[:, :, None, None], ids.shape + (1, LANE)).astype(jnp.int32)
 
     scratch = whole_scratch(sizes, CHUNKS, capacity, width, per_owner, block)
     held, gram, basis = call(

time: 185 us -> 183 us (0.989)
  Pallas kernels: 181 us -> 179 us
    pallas_call x2, Pallas kernels: 181 us -> 179 us  [call(): pl.pallas_call(body, out_shape=[jax.ShapeDtypeStruct(shape, kind) for sha...]
where the time goes in v3:
time: 183 us
  Pallas kernels  179 us (98%)
  local copies, waits for them, and re-layouts  2.14 us (1%)
    pallas_call x2, Pallas kernels, call(): pl.pallas_call(body, out_shape=[jax.ShapeDtypeStruct(shape, kind) for sha...  179 us

profile of v3, /device:TPU:1, one launch (start us, length us, event | category | flops | bytes accessed | tf_op | source)
XLA Modules:
  0.0 182.7 jit_solution(12846307876751355208)
XLA Ops:
  1.3 0.0 copy-start
  1.3 0.7 copy-done
  2.0 0.1 select_reduce_fusion.3
  2.1 0.1 select_reduce_fusion
  2.2 0.6 concatenate.3.info_ref
  2.8 0.1 reshape.44
  2.9 0.1 copy.9
  3.0 0.7 broadcast_in_dim.80.ids_ref
  3.7 175.4 %shard_map.67 = (f32[2,64,128]{2,1,0:T(8,128)}, f32[32,128]{1,0:T(8,128)}, bf16[64,1024]{1,0:T(8,128)(2,1)}) custom-call(s32[112]{0:T(128)} %concatenate.3.info_ref, s32[4,8,1,128]{3,2,1,0:T(1,128)} %broadcast_in_dim.80.ids_ref, f32[16,128,128]{2,1,0:T(8,128)} %tiles_hbm.1, bf16[64,1024]{1,0:T(8,128)(2,1)} %bitcast.17), custom_call_target="tpu_custom_call" | custom-call | tf_op jit(solution)/shard_map/pallas_call | solution.py:749
  179.1 3.6 %shard_map.68 = (f32[64,256]{1,0:T(8,128)}, bf16[64,1024]{1,0:T(8,128)(2,1)}, f32[64,64]{1,0:T(8,128)}) custom-call(f32[32,128]{1,0:T(8,128)} %get-tuple-element.9.gram_ref, f32[2,64,128]{2,1,0:T(8,128)} %get-tuple-element.10.held_ref, bf16[64,1024]{1,0:T(8,128)(2,1)} %get-tuple-element.11.basis_ref), custom_call_target="tpu_custom_call" | custom-call | tf_op jit(solution)/shard_map/pallas_call | solution.py:749
  (6 shorter events, 0.1 us)
Async XLA Ops:
  1.3 0.7 copy-start

commit v4 on v3

--- a/solution.py
+++ b/solution.py
@@ -14,7 +14,7 @@
 LANE = 128
 CORES = 2
 CHUNKS = 2
-TOGETHER = 8
+TOGETHER = 16
 
 
 def nn(left, right):
@@ -55,17 +55,14 @@
 
 def greet(sizes, row, col):
     n_row, n_col, nx = sizes
-    nz = n_row // nx
-    z, x = row // nx, lax.rem(row, nx)
     barrier = pltpu.get_barrier_semaphore()
 
     def signal(device):
         pl.semaphore_signal(barrier, inc=1, device_id=device, device_id_type=MESH)
 
-    loop(1, nx, lambda d: signal((z * nx + lax.rem(x + d, nx), col)))
-    loop(1, nz, lambda d: signal((lax.rem(z + d, nz) * nx + x, col)))
+    loop(1, n_row, lambda d: signal((lax.rem(row + d, n_row), col)))
     loop(1, n_col, lambda d: signal((row, lax.rem(col + d, n_col))))
-    pl.semaphore_wait(barrier, nx + nz + n_col - 3)
+    pl.semaphore_wait(barrier, n_row + n_col - 2)
 
 
 class Exchange:
@@ -83,6 +80,8 @@
         loop(0, self.n - 1, self.start_one)
 
     def wait(self):
+        if self.n == 1:
+            return
         everything = self.dst.at[pl.ds(0, self.n - 1)]
         device = self.device(lax.rem(self.me + 1, self.n))
         remote(everything, everything, self.send, self.recv, device).wait()
@@ -193,102 +192,103 @@
 class RowExchange:
     def __init__(self, sizes, row, col, out, r, tag):
         n_row, n_col, nx = sizes
-        nz = n_row // nx
-        z, x = row // nx, lax.rem(row, nx)
-        self.nx, self.nz, self.x, self.z, self.out = nx, nz, x, z, out
-        self.mid, self.got = r[tag + "mid"], r[tag + "got"]
-        self.along_x = Exchange(
-            nx,
-            x,
-            lambda p: out.at[p],
-            None,
-            r[tag + "x_send"],
-            r[tag + "x_recv"],
-            lambda p: (z * nx + p, col),
-        )
-        self.along_z = Exchange(
-            nz,
-            z,
-            lambda p: self.mid.at[p],
-            self.got,
-            r[tag + "z_send"],
-            r[tag + "z_recv"],
-            lambda p: (p * nx + x, col),
-        )
-
-    def x_peer(self, k):
-        return lax.rem(self.x + offset(k, self.nx), self.nx)
-
-    def send_x(self, k):
-        e = self.along_x
-        peer = self.x_peer(k)
+        self.n_row, self.nx, self.nz = n_row, nx, n_row // nx
+        self.z, self.x, self.row, self.col, self.out = row // nx, lax.rem(row, nx), row, col, out
+        self.got, self.send, self.recv = r[tag + "got"], r[tag + "send"], r[tag + "recv"]
+        self.relayed = 0
+        if tag + "relay_out" in r:
+            self.relayed = nx // 2
+            self.relay_out, self.relay_in = r[tag + "relay_out"], r[tag + "relay_in"]
+            self.relay = remote(
+                self.relay_out,
+                self.relay_in,
+                r[tag + "relay_send"],
+                r[tag + "relay_recv"],
+                (self.member(self.nz - 1, 0), col),
+            )
+
+    def member(self, dz, dx):
+        return lax.rem(self.z + dz, self.nz) * self.nx + lax.rem(self.x + dx, self.nx)
+
+    def direct(self, p):
         remote(
-            self.out.at[peer], self.mid.at[:, self.x], e.send, e.recv, e.device(peer)
+            self.out.at[p], self.got.at[self.row], self.send, self.recv, (p, self.col)
         ).start()
 
-    def turn(self):
-        e = self.along_x
-        everything = self.out.at[pl.ds(0, self.nx - 1)]
-        remote(everything, everything, e.send, e.recv, e.device(self.x_peer(0))).wait()
-        self.along_z.start()
-        self.got[self.z] = self.mid[self.z]
+    def start(self, store=None):
+        nx, nz = self.nx, self.nz
+        half = nz // 2
+
+        def serve(p):
+            if store is not None:
+                store("out", p, p)
+            self.direct(p)
+
+        if self.relayed:
+            if store is not None:
+                for j in range(self.relayed):
+                    store("relay_out", j, self.member(half, nx - self.relayed + j))
+            self.relay.start()
+        loop(0, nx - self.relayed, lambda j: serve(self.member(half, j)))
+
+        def other(k):
+            q = k // nx
+            distance = half - 1 - q // 2
+            ahead = 1 - 2 * lax.rem(q, 2)
+            serve(self.member(nz + distance * ahead, lax.rem(k, nx)))
+
+        loop(0, (nz - 2) * nx, other)
+        loop(1, nx, lambda j: serve(self.member(0, j)))
+        if store is not None:
+            store("got", self.row, self.row)
+
+    def forward(self):
+        self.relay.wait()
+        source = self.member(1, 0)
+        for j in range(self.relayed):
+            target = self.member(1 + self.nz // 2, self.nx - self.relayed + j)
+            remote(
+                self.relay_in.at[j], self.got.at[source], self.send, self.recv, (target, self.col)
+            ).start()
 
     def wait(self):
-        self.along_z.wait()
-
-
-def exchange_scratch(sizes, tag, shape, kind, out=True):
+        everything = self.got.at[pl.ds(0, self.n_row - 1)]
+        remote(everything, everything, self.send, self.recv, (self.member(1, 0), self.col)).wait()
+
+
+def exchange_scratch(sizes, tag, shape, kind, plain=False):
     n_row, n_col, nx = sizes
-    nz = n_row // nx
-    named = {
-        tag + "mid": pltpu.VMEM((nz, nx) + shape, kind),
-        tag + "got": pltpu.VMEM((nz, nx) + shape, kind),
-    }
-    if out:
-        named[tag + "out"] = pltpu.VMEM((nx, nz) + shape, kind)
-    for name in ("x_send", "x_recv", "z_send", "z_recv"):
-        named[tag + name] = pltpu.SemaphoreType.DMA
+    dma = pltpu.SemaphoreType.DMA
+    named = {tag + "got": pltpu.VMEM((n_row,) + shape, kind), tag + "send": dma, tag + "recv": dma}
+    if not plain:
+        named[tag + "out"] = pltpu.VMEM((n_row,) + shape, kind)
+        named[tag + "relay_out"] = pltpu.VMEM((nx // 2,) + shape, kind)
+        named[tag + "relay_in"] = pltpu.VMEM((nx // 2,) + shape, kind)
+        named[tag + "relay_send"] = dma
+        named[tag + "relay_recv"] = dma
     return named
 
 
 class Spread:
     def __init__(self, sizes, row, col, chunks, r, tag):
         tags = [tag + "%d" % c for c in range(chunks)]
-        self.chunks, self.wanted = chunks, r["wanted_got"]
+        self.wanted = r["wanted_got"]
         self.moves = [RowExchange(sizes, row, col, r[t + "out"], r, t) for t in tags]
         self.got = [move.got for move in self.moves]
 
     def start(self, own_ref):
-        first = self.moves[0]
-        rows = own_ref.shape[0] // self.chunks
-
-        def column(peer, store):
-            def one(p):
-                block = pick(own_ref[...], self.wanted[p, peer])
-                for c in range(self.chunks):
-                    store(self.moves[c], p, block[c * rows : (c + 1) * rows])
-
-            loop(0, first.nz, one)
-
-        def away(k):
-            peer = first.x_peer(k)
-
-            def store(move, p, block):
-                move.out[peer, p] = block
-
-            column(peer, store)
-            first.send_x(k)
-
-        def here(move, p, block):
-            move.mid[p, move.x] = block
-
-        loop(0, first.nx - 1, away)
-        column(first.x, here)
-        for c in range(self.chunks):
-            if c:
-                loop(0, first.nx - 1, self.moves[c].send_x)
-        for c in range(self.chunks):
-            self.moves[c].turn()
+        rows = own_ref.shape[0] // len(self.moves)
+
+        def store(kind, slot, p):
+            block = pick(own_ref[...], self.wanted[p])
+            for c, move in enumerate(self.moves):
+                getattr(move, kind)[slot] = block[c * rows : (c + 1) * rows]
+
+        self.moves[0].start(store)
+        for move in self.moves[1:]:
+            move.start()
+        for move in self.moves:
+            move.forward()
 
 
 class RowSums:
@@ -331,11 +331,9 @@
     def sketch(self, got, splits, info):
         capacity = splits[0].shape[0]
         dims = (((1,), (1,)), ((), ()))
-        nx = got.shape[1]
 
         def multiply(t):
-            owner = info["owner"](t)
-            block = got[owner // nx, lax.rem(owner, nx)]
+            block = got[info["owner"](t)]
             total = lax.dot_general(block, splits[2][t], dims, preferred_element_type=f32)
             total += lax.dot_general(block, splits[1][t], dims, preferred_element_type=f32)
             total += lax.dot_general(block, splits[0][t], dims, preferred_element_type=f32)
@@ -452,20 +450,10 @@
         each_tile(capacity, multiply)
         self.terms[capacity] = jnp.zeros(self.terms.shape[1:], f32)
 
-        def away(k):
-            peer = move.x_peer(k)
-
-            def one(p):
-                move.out[peer, p] = self.terms[info["slot"](p * move.nx + peer)]
-
-            loop(0, move.nz, one)
-            move.send_x(k)
-
-        def here(p):
-            move.mid[p, move.x] = self.terms[info["slot"](p * move.nx + move.x)]
-
-        loop(0, move.nx - 1, away)
-        loop(0, move.nz, here)
+        def store(kind, slot, p):
+            getattr(move, kind)[slot] = self.terms[info["slot"](p)]
+
+        move.start(store)
 
     def finish(self, columns_ref, first):
         move = self.move
@@ -473,14 +461,15 @@
         rows = self.terms.shape[1]
 
         def column(b):
-            def add(p, total):
-                for q in range(move.nx):
-                    hit = jnp.broadcast_to(self.wanted[p, q], (rows, LANE)) == b + 1
-                    total = total + jnp.where(hit, move.got[p, q], 0.0)
+            def add(q, total):
+                for j in range(4):
+                    p = 4 * q + j
+                    hit = jnp.broadcast_to(self.wanted[p], (rows, LANE)) == b + 1
+                    total = total + jnp.where(hit, move.got[p], 0.0)
                 return total
 
             columns_ref[b, first : first + rows] = lax.fori_loop(
-                0, move.nz, add, jnp.zeros((rows, LANE), f32)
+                0, move.n_row // 4, add, jnp.zeros((rows, LANE), f32)
             )
 
         loop(0, columns_ref.shape[0], column)
@@ -555,13 +544,8 @@
 
     greet(sizes, row, col)
     ids = RowExchange(sizes, row, col, ids_ref, r, "wanted_")
-    loop(0, nx - 1, ids.send_x)
-
-    def own_id(p):
-        ids.mid[p, ids.x] = ids_ref[ids.x, p]
-
-    loop(0, ids.nz, own_id)
-    ids.turn()
+    ids.start()
+    ids.got[row] = ids_ref[row]
 
     def split(t):
         for ref, piece in zip(splits, three(tiles_ref[t])):
@@ -594,20 +578,20 @@
         sums[c].pair_up()
         if c >= 2:
             send_terms(c - 2)
-            moves[c - 2].move.turn()
+            moves[c - 2].move.forward()
     last = chunks - 1
     if last >= 1:
         send_terms(last - 1)
     gather(last)
     if last >= 1:
-        moves[last - 1].move.turn()
+        moves[last - 1].move.forward()
     gram_one.scatter_x(pack_gram(held[0]) + pack_gram(held[1]))
     gram_one.sum_z()
     sums[last].gathered()
     gram_one.sum_columns()
     moves[last].start(sums[last].group, splits, info)
+    moves[last].move.forward()
     gram_one.gather_x()
-    moves[last].move.turn()
     loop_factor(gram_one.result(), total_rows, work)
     inverse_one = inverse_of(work)
     for c in range(chunks):
@@ -669,7 +653,7 @@
     }
     for tag in ("gram_one_", "gram_cols_", "gram_two_"):
         named.update(gram_scratch(sizes, tag))
-    named.update(exchange_scratch(sizes, "wanted_", (1, LANE), jnp.int32, out=False))
+    named.update(exchange_scratch(sizes, "wanted_", (1, LANE), jnp.int32, True))
     rows = width // chunks
     for c in range(chunks):
         for tag, kind in (("one_", bf16), ("two_", bf16), ("sum", f32)):
@@ -790,8 +774,7 @@
     ).astype(jnp.int32)
     match = (owner[:, None] == owners[None, :]) & live[:, None]
     ids = jnp.sum(jnp.where(match, within[:, None] + 1, 0), axis=0)
-    ids = ids.reshape(n_row // nx, nx).T
-    ids = jnp.broadcast_to(ids[:, :, None, None], ids.shape + (1, LANE)).astype(jnp.int32)
+    ids = jnp.broadcast_to(ids[:, None, None], (n_row, 1, LANE)).astype(jnp.int32)
 
     scratch = whole_scratch(sizes, CHUNKS, capacity, width, per_owner, block)
     held, gram, basis = call(

time: 183 us -> 173 us (0.945)
  Pallas kernels: 179 us -> 169 us
    pallas_call x2, Pallas kernels: 179 us -> 169 us  [call(): pl.pallas_call(body, out_shape=[jax.ShapeDtypeStruct(shape, kind) for sha...]
where the time goes in v4:
time: 173 us
  Pallas kernels  169 us (98%)
  local copies, waits for them, and re-layouts  1.97 us (1%)
    pallas_call x2, Pallas kernels, call(): pl.pallas_call(body, out_shape=[jax.ShapeDtypeStruct(shape, kind) for sha...  169 us

profile of v4, /device:TPU:1, one launch (start us, length us, event | category | flops | bytes accessed | tf_op | source)
XLA Modules:
  0.0 172.9 jit_solution(18370437574852723536)
XLA Ops:
  1.3 0.0 copy-start
  1.3 0.7 copy-done
  2.0 0.1 select_reduce_fusion.3
  2.1 0.1 select_reduce_fusion
  2.2 0.6 concatenate.3.info_ref
  2.8 0.7 broadcast_in_dim.80.ids_ref
  3.5 165.8 %shard_map.67 = (f32[2,64,128]{2,1,0:T(8,128)}, f32[32,128]{1,0:T(8,128)}, bf16[64,1024]{1,0:T(8,128)(2,1)}) custom-call(s32[112]{0:T(128)} %concatenate.3.info_ref, s32[32,1,128]{2,1,0:T(1,128)} %broadcast_in_dim.80.ids_ref, f32[16,128,128]{2,1,0:T(8,128)} %tiles_hbm.1, bf16[64,1024]{1,0:T(8,128)(2,1)} %bitcast.16), custom_call_target="tpu_custom_call" | custom-call | tf_op jit(solution)/shard_map/pallas_call | solution.py:733
  169.3 3.6 %shard_map.68 = (f32[64,256]{1,0:T(8,128)}, bf16[64,1024]{1,0:T(8,128)(2,1)}, f32[64,64]{1,0:T(8,128)}) custom-call(f32[32,128]{1,0:T(8,128)} %get-tuple-element.9.gram_ref, f32[2,64,128]{2,1,0:T(8,128)} %get-tuple-element.10.held_ref, bf16[64,1024]{1,0:T(8,128)(2,1)} %get-tuple-element.11.basis_ref), custom_call_target="tpu_custom_call" | custom-call | tf_op jit(solution)/shard_map/pallas_call | solution.py:733
  (6 shorter events, 0.1 us)
Async XLA Ops:
  1.3 0.7 copy-start

commit v5 on v1

--- a/solution.py
+++ b/solution.py
@@ -77,27 +77,20 @@
 
 
 class Exchange:
-    def __init__(self, n, me, source, dst, send, recv, device):
+    def __init__(self, n, me, source, dst, send, recv, device, each=False):
         self.n, self.me, self.source, self.dst = n, me, source, dst
-        self.send, self.recv, self.device = send, recv, device
+        self.send, self.recv, self.device, self.each = send, recv, device, each
+
+    def copy(self, peer, slot):
+        send = self.send.at[peer] if self.each else self.send
+        recv = self.recv.at[slot] if self.each else self.recv
+        return remote(self.source(peer), self.dst.at[slot], send, recv, self.device(peer))
 
     def copy_to(self, peer):
-        return remote(
-            self.source(peer),
-            self.dst.at[self.me],
-            self.send.at[peer],
-            self.recv.at[self.me],
-            self.device(peer),
-        )
+        return self.copy(peer, self.me)
 
     def copy_from(self, peer):
-        return remote(
-            self.source(peer),
-            self.dst.at[peer],
-            self.send.at[peer],
-            self.recv.at[peer],
-            self.device(peer),
-        )
+        return self.copy(peer, peer)
 
     def start(self):
         loop(
@@ -105,11 +98,11 @@
         )
 
     def wait(self):
-        loop(
-            0,
-            self.n - 1,
-            lambda k: self.copy_from(lax.rem(self.me - offset(k, self.n) + self.n, self.n)).wait(),
-        )
+        if self.n == 1:
+            return
+        everything = self.dst.at[pl.ds(0, self.n - 1)]
+        device = self.device(lax.rem(self.me + 1, self.n))
+        remote(everything, everything, self.send, self.recv, device).wait()
 
 
 def sum_slots(ref, n):
@@ -119,13 +112,13 @@
     return total
 
 
-def pack_gram(block):
-    size = block.shape[0]
-    half = size // 2
-    zero = jnp.zeros_like(block)
-    return nt(block[:half], jnp.concatenate([block, zero], axis=0)) + nt(
-        block[half:], jnp.concatenate([zero, block], axis=0)
-    )
+def gram_of(block):
+    return nt(block, jnp.concatenate([block, jnp.zeros_like(block)], axis=0))
+
+
+def pack_gram(gram):
+    half = gram.shape[0] // 2
+    return gram[:half] + pltpu.roll(gram[half:], 64, 1)
 
 
 class GramSum:
@@ -194,14 +187,14 @@
         "s2": pltpu.VMEM((depth, LANE), f32),
         "gc": pltpu.VMEM((n_col, depth, LANE), f32),
         "out": pltpu.VMEM((nx, depth, LANE), f32),
-        "x_send": dma((nx,)),
-        "x_recv": dma((nx,)),
-        "z_send": dma((nz,)),
-        "z_recv": dma((nz,)),
-        "c_send": dma((n_col,)),
-        "c_recv": dma((n_col,)),
-        "o_send": dma((nx,)),
-        "o_recv": dma((nx,)),
+        "x_send": dma,
+        "x_recv": dma,
+        "z_send": dma,
+        "z_recv": dma,
+        "c_send": dma,
+        "c_recv": dma,
+        "o_send": dma,
+        "o_recv": dma,
     }
     return {tag + name: shape for name, shape in named.items()}
 
@@ -229,6 +222,7 @@
                 r[tag + "send%d" % c],
                 r[tag + "recv%d" % c],
                 lambda p: (p, col),
+                c + 1 < chunks,
             )
             for c in range(chunks)
         ]
@@ -250,11 +244,14 @@
         self.store(self.got, self.row, pick(own_ref[...], self.wanted[self.row]))
 
     def finish(self, c):
+        if c + 1 == self.chunks:
+            self.moves[c].wait()
+            return
+
         def step(k):
             peer = lax.rem(self.row - offset(k, self.n_row) + self.n_row, self.n_row)
             self.moves[c].copy_from(peer).wait()
-            if c + 1 < self.chunks:
-                self.moves[c + 1].copy_to(peer).start()
+            self.moves[c + 1].copy_to(peer).start()
 
         loop(0, self.n_row - 1, step)
 
@@ -265,8 +262,9 @@
     for c in range(chunks):
         named[tag + "outgoing%d" % c] = pltpu.VMEM((n_row, rows, LANE), bf16)
         named[tag + "got%d" % c] = pltpu.VMEM((n_row, rows, LANE), bf16)
-        named[tag + "send%d" % c] = pltpu.SemaphoreType.DMA((n_row,))
-        named[tag + "recv%d" % c] = pltpu.SemaphoreType.DMA((n_row,))
+        for name in ("send%d", "recv%d"):
+            each = pltpu.SemaphoreType.DMA((n_row,))
+            named[tag + name % c] = each if c + 1 < chunks else pltpu.SemaphoreType.DMA
     return named
 
 
@@ -403,7 +401,8 @@
             "summed": pltpu.VMEM((ny, 2, rows, LANE), f32),
             "far": pltpu.VMEM((ny, 2, rows, LANE), f32),
         }
-        sems = ["near_send", "near_recv", "far_send", "far_recv"]
+        some["far_send"] = some["far_recv"] = dma
+        sems = ["near_send", "near_recv"]
         if gather:
             some["group"] = pltpu.VMEM((n_col, 2, rows, LANE), f32)
             sems += ["all_send", "all_recv", "pass_send", "pass_recv"]
@@ -473,12 +472,15 @@
         rows = self.arrived.shape[1]
 
         def column(b):
-            def add(s, total):
-                hit = jnp.broadcast_to(self.wanted[s], (rows, LANE)) == b + 1
-                return total + jnp.where(hit, self.arrived[s], 0.0)
+            def add(q, total):
+                for j in range(8):
+                    s = 8 * q + j
+                    hit = jnp.broadcast_to(self.wanted[s], (rows, LANE)) == b + 1
+                    total = total + jnp.where(hit, self.arrived[s], 0.0)
+                return total
 
             columns_ref[b, first : first + rows] = lax.fori_loop(
-                0, self.n_row, add, jnp.zeros((rows, LANE), f32)
+                0, self.n_row // 8, add, jnp.zeros((rows, LANE), f32)
             )
 
         loop(0, columns_ref.shape[0], column)
@@ -491,8 +493,8 @@
         named["terms%d" % c] = pltpu.VMEM((capacity + 1, rows, LANE), f32)
         named["leaving%d" % c] = pltpu.VMEM((n_row, rows, LANE), f32)
         named["arrived%d" % c] = pltpu.VMEM((n_row, rows, LANE), f32)
-        named["leaving_send%d" % c] = pltpu.SemaphoreType.DMA((n_row,))
-        named["leaving_recv%d" % c] = pltpu.SemaphoreType.DMA((n_row,))
+        named["leaving_send%d" % c] = pltpu.SemaphoreType.DMA
+        named["leaving_recv%d" % c] = pltpu.SemaphoreType.DMA
     return named
 
 
@@ -568,6 +570,7 @@
         r["id_send"],
         r["id_recv"],
         lambda p: (p, col),
+        True,
     )
     ids.start()
     wanted[row] = ids_ref[row]
@@ -581,41 +584,46 @@
     spread = Spread(n_row, row, col, chunks, r, "one_")
     sums = [RowSums(n_col, row, col, c, r, "one_") for c in range(chunks)]
     spread.start(own_ref, lambda peer: ids.copy_from(peer).wait())
+    gram_one = GramSum(sizes, row, col, r, "gram_one_")
+    moves = [ColumnSums(n_row, row, col, c, r) for c in range(chunks)]
+
+    def gather(c):
+        total = sums[c].total()
+        sums[c].gather(total)
+        held[:, c * rows : (c + 1) * rows] = total
+
+    def send_terms(c):
+        sums[c].gathered()
+        moves[c].start(sums[c].group, splits, info)
+
     for c in range(chunks):
         spread.finish(c)
         sums[c].sketch(spread.got[c], splits, info)
         sums[c].start()
+        if c >= 1:
+            gather(c - 1)
         sums[c].pair_up()
-    for c in range(chunks):
-        total = sums[c].total()
-        sums[c].gather(total)
-        held[:, c * rows : (c + 1) * rows] = total
-    gram_one = GramSum(sizes, row, col, r, "gram_one_")
-    gram_one.scatter_x(pack_gram(held[0]) + pack_gram(held[1]))
-    moves = [ColumnSums(n_row, row, col, c, r) for c in range(chunks)]
-    steps = [gram_one.sum_z, gram_one.sum_columns, gram_one.gather_x]
-    for c in range(chunks):
-        sums[c].gathered()
-        if c + 1 == chunks:
-            for step in steps[1:]:
-                step()
-        elif c == 0:
-            steps[0]()
-        moves[c].start(sums[c].group, splits, info)
-    if chunks == 1:
-        for step in steps:
-            step()
+        if c >= 1:
+            send_terms(c - 1)
+    last = chunks - 1
+    gather(last)
+    gram_one.scatter_x(pack_gram(gram_of(held[0]) + gram_of(held[1])))
+    gram_one.sum_z()
+    gram_one.sum_columns()
+    sums[last].gathered()
+    gram_one.gather_x()
+    moves[last].start(sums[last].group, splits, info)
     loop_factor(gram_one.result(), total_rows, work)
     inverse_one = inverse_of(work)
     for c in range(chunks):
         moves[c].finish(columns_ref, c * rows)
 
-    def normalise(b, packed):
+    total = jnp.zeros((width, LANE), f32)
+    for b in range(columns_ref.shape[0]):
         block = apply_inverse(inverse_one, columns_ref[b])
         columns_ref[b] = block
-        return packed + pack_gram(block)
-
-    packed = lax.fori_loop(0, columns_ref.shape[0], normalise, jnp.zeros((32, LANE), f32))
+        total = total + gram_of(block)
+    packed = pack_gram(total)
     gram_cols = GramSum(sizes, row, col, r, "gram_cols_")
     gram_cols.scatter_x(packed)
     gram_cols.sum_z()
@@ -639,7 +647,7 @@
     for c in range(chunks):
         held_ref[:, c * rows : (c + 1) * rows] = sums[c].total()
     gram_two = GramSum(sizes, row, col, r, "gram_two_")
-    gram_two.scatter_x(pack_gram(held_ref[0]) + pack_gram(held_ref[1]))
+    gram_two.scatter_x(pack_gram(gram_of(held_ref[0]) + gram_of(held_ref[1])))
     gram_two.sum_z()
     gram_two.sum_columns()
     gram_two.gather_x()

time: 164 us -> 161 us (0.982)
  Pallas kernels: 159 us -> 157 us
    pallas_call x2, Pallas kernels: 159 us -> 157 us  [call(): pl.pallas_call(body, out_shape=[jax.ShapeDtypeStruct(shape, kind) for sha...]
where the time goes in v5:
time: 161 us
  Pallas kernels  157 us (98%)
  local copies, waits for them, and re-layouts  2.97 us (2%)
    pallas_call x2, Pallas kernels, call(): pl.pallas_call(body, out_shape=[jax.ShapeDtypeStruct(shape, kind) for sha...  157 us

profile of v5, /device:TPU:1, one launch (start us, length us, event | category | flops | bytes accessed | tf_op | source)
XLA Modules:
  0.0 161.2 jit_solution(14603324159171882188)
XLA Ops:
  1.3 0.0 copy-start.2
  1.3 0.7 copy-done.2
  2.0 0.1 select_reduce_fusion.3
  2.1 0.1 select_reduce_fusion
  2.2 0.1 concatenate.3.info_ref
  2.3 0.1 broadcast_in_dim.80.ids_ref
  2.4 0.0 copy-start
  2.4 1.2 copy-done
  3.6 0.0 copy-start.1
  3.7 0.9 copy-done.1
  4.6 154.0 %shard_map.67 = (f32[2,64,128]{2,1,0:T(8,128)S(1)}, f32[32,128]{1,0:T(8,128)S(1)}, bf16[64,1024]{1,0:T(8,128)(2,1)S(1)}) custom-call(s32[112]{0:T(128)S(1)} %concatenate.3.info_ref, f32[16,128,128]{2,1,0:T(8,128)S(1)} %copy-done, bf16[64,1024]{1,0:T(8,128)(2,1)S(1)} %bitcast.16, s32[32,1,128]{2,1,0:T(1,128)S(1)} %broadcast_in_dim.80.ids_ref), custom_call_target="tpu_custom_call" | custom-call | tf_op jit(solution)/shard_map/pallas_call | solution.py:746
  158.5 2.6 %shard_map.68 = (f32[64,256]{1,0:T(8,128)}, bf16[64,1024]{1,0:T(8,128)(2,1)}, f32[64,64]{1,0:T(8,128)}) custom-call(f32[32,128]{1,0:T(8,128)S(1)} %get-tuple-element.9.gram_ref, f32[2,64,128]{2,1,0:T(8,128)S(1)} %get-tuple-element.10.held_ref, bf16[64,1024]{1,0:T(8,128)(2,1)S(1)} %get-tuple-element.11.basis_ref), custom_call_target="tpu_custom_call" | custom-call | tf_op jit(solution)/shard_map/pallas_call | solution.py:746
  (6 shorter events, 0.1 us)
Async XLA Ops:
  1.3 0.7 copy-start.2
  2.4 1.2 copy-start
  3.6 0.9 copy-start.1

commit v6 on v5

--- a/solution.py
+++ b/solution.py
@@ -629,8 +629,8 @@
     gram_cols.sum_z()
     gram_cols.sum_columns()
     gram_cols.gather_x()
-    loop_factor(gram_cols.result(), total_cols, work)
-    inverse_cols = inverse_of(work)
+    gram_cols.last.wait()
+    unused, inverse_cols = split_factor(factor(gram_cols.out, total_cols))
     for b in range(columns_ref.shape[0]):
         basis_ref[:, b * LANE : (b + 1) * LANE] = apply_inverse(inverse_cols, columns_ref[b]).astype(
             bf16

time: 161 us -> 161 us (level)
  no operation moved by 1% of the time
where the time goes in v6:
time: 161 us; the launch traced here: 160 us
  Pallas kernels  156 us (97%)
  local copies, waits for them, and re-layouts  2.97 us (2%)
    pallas_call x2, Pallas kernels, call(): pl.pallas_call(body, out_shape=[jax.ShapeDtypeStruct(shape, kind) for sha...  156 us

profile of v6, /device:TPU:1, one launch (start us, length us, event | category | flops | bytes accessed | tf_op | source)
XLA Modules:
  0.0 160.4 jit_solution(11186836418995962296)
XLA Ops:
  1.3 0.0 copy-start.2
  1.3 0.7 copy-done.2
  2.0 0.1 select_reduce_fusion.3
  2.1 0.1 select_reduce_fusion
  2.2 0.1 concatenate.3.info_ref
  2.3 0.1 broadcast_in_dim.80.ids_ref
  2.4 0.0 copy-start
  2.4 1.2 copy-done
  3.6 0.0 copy-start.1
  3.7 0.9 copy-done.1
  4.6 153.2 %shard_map.67 = (f32[2,64,128]{2,1,0:T(8,128)S(1)}, f32[32,128]{1,0:T(8,128)S(1)}, bf16[64,1024]{1,0:T(8,128)(2,1)S(1)}) custom-call(s32[112]{0:T(128)S(1)} %concatenate.3.info_ref, f32[16,128,128]{2,1,0:T(8,128)S(1)} %copy-done, bf16[64,1024]{1,0:T(8,128)(2,1)S(1)} %bitcast.16, s32[32,1,128]{2,1,0:T(1,128)S(1)} %broadcast_in_dim.80.ids_ref), custom_call_target="tpu_custom_call" | custom-call | tf_op jit(solution)/shard_map/pallas_call | solution.py:746
  157.8 2.6 %shard_map.68 = (f32[64,256]{1,0:T(8,128)}, bf16[64,1024]{1,0:T(8,128)(2,1)}, f32[64,64]{1,0:T(8,128)}) custom-call(f32[32,128]{1,0:T(8,128)S(1)} %get-tuple-element.9.gram_ref, f32[2,64,128]{2,1,0:T(8,128)S(1)} %get-tuple-element.10.held_ref, bf16[64,1024]{1,0:T(8,128)(2,1)S(1)} %get-tuple-element.11.basis_ref), custom_call_target="tpu_custom_call" | custom-call | tf_op jit(solution)/shard_map/pallas_call | solution.py:746
  (6 shorter events, 0.1 us)
Async XLA Ops:
  1.3 0.7 copy-start.2
  2.4 1.2 copy-start
  3.6 0.9 copy-start.1
